TPU v7x, 256 devices: a whole 4x4x8 slice. The times are simulated.
256 devices in a mesh: tensor: 32 (over y, x, z_lo), section: 8 (over z_hi, core).
Axes of the slice: x: 4, y: 4, z: 8 (z_hi: 4, z_lo: 2; z = z_hi * 2 + z_lo), core: 2. Of those that a mesh axis runs over, the one named last changes fastest.
Arguments:
- resid: bfloat16 [8, 384, 8192], P('section', 'tensor'), may hold values from -6 to 6
- norm_gain: float32 [8192], replicated, may hold values from 0.1 to 1.9
- signs: int32 [8192], replicated, may hold values from 0 to 1
- query_weight: bfloat16 [8192, 8192], P(None, 'tensor'), may hold values from -0.30935922 to 0.30935922
- kv_weight: bfloat16 [8192, 2048], P(None, 'tensor'), may hold values from -0.30935922 to 0.30935922
- out_weight: bfloat16 [8192, 8192], P('tensor'), may hold values from -0.25 to 0.25
- lengths: int32 [8], replicated, may hold values from 1 to 384, 2304 in all
Outputs:
- mixed: bfloat16 [8, 384, 8192], P('section', 'tensor')
Inputs may be any that keep to these rules, and one draw needn't show every extreme that they name: Block c holds lengths[c] valid tokens at its start and padding after them; the lengths sum to 2304 and at least one block is full.
All inputs are finite; a program needn't handle non-finite values.
Results may differ from a plain program's by a relative error of at most 0.025.
Values may be sent and summed in bfloat16 or wider, within the bound.
A program may use at most 128 MiB of HBM per device.

v0:
```python
import math

import jax
import jax.numpy as jnp
from jax import lax
from jax.sharding import PartitionSpec as P

KVH = 8
HD = 128
HB = 128


rope_base = 500000.0
norm_eps = 1e-05


def hadamard_table(extent):
    index = jnp.arange(extent, dtype=jnp.int32)
    parity = jnp.zeros((extent, extent), jnp.int32)
    bit_value = 1
    while bit_value < extent:
        row_bit = index // bit_value % 2
        parity = parity + row_bit[:, None] * row_bit[None, :]
        bit_value = bit_value * 2
    return (1 - 2 * (parity % 2)).astype(jnp.float32)


def rotate_blocks(values, sign_row, hadamard):
    row_count = values.shape[0]
    grouped = (values * sign_row).reshape(row_count, -1, hadamard.shape[0])
    result = jnp.einsum("rbj,ji->rbi", grouped, hadamard, precision=lax.Precision.HIGHEST)
    return result.reshape(row_count, -1) / math.sqrt(hadamard.shape[0])


def unrotate_blocks(values, sign_row, hadamard):
    row_count = values.shape[0]
    grouped = values.reshape(row_count, -1, hadamard.shape[0])
    result = jnp.einsum("rbi,ji->rbj", grouped, hadamard, precision=lax.Precision.HIGHEST)
    return result.reshape(row_count, -1) / math.sqrt(hadamard.shape[0]) * sign_row


def inverse_freqs(head_dim):
    return jnp.exp(
        jnp.arange(head_dim // 2, dtype=jnp.float32) * (-2.0 * math.log(rope_base) / head_dim)
    )


def rotary(inputs, float_pos):
    half_dim = inputs.shape[-1] // 2
    angles = float_pos[:, None] * inverse_freqs(inputs.shape[-1])[None, :]
    cosine = jnp.cos(angles)[:, None, :]
    sine_part = jnp.sin(angles)[:, None, :]
    first_half = inputs[..., :half_dim]
    second_half = inputs[..., half_dim:]
    return jnp.concatenate(
        [
            first_half * cosine - second_half * sine_part,
            second_half * cosine + first_half * sine_part,
        ],
        axis=-1,
    )


def swap_halves(inputs, quarters):
    middle = quarters // 2
    return jnp.concatenate([-inputs[:, middle:], inputs[:, :middle]], axis=1)


def absorb(carry, scores, visible, combine):
    row_max, row_total, running = carry
    masked = visible[None, None]
    new_max = jnp.maximum(row_max, jnp.max(jnp.where(masked, scores, -1e30), axis=-1))
    weights = jnp.where(masked, jnp.exp(scores - new_max[..., None]), 0.0)
    new_total = jnp.sum(weights, axis=-1)
    new_running = combine(weights.astype(jnp.bfloat16))
    return (new_max, new_total, new_running)


def shards(resid, norm_gain, signs, query_weight, kv_weight, out_weight, lengths):
    tensor_count = lax.axis_size("tensor")
    section_count = lax.axis_size("section")
    tensor_here = lax.axis_index("tensor")
    section_here = lax.axis_index("section")
    rows_here = resid.shape[1]
    width = resid.shape[2]
    block_len = rows_here * tensor_count
    heads_here = query_weight.shape[1] // HD
    heads_all = heads_here * tensor_count
    group_size = heads_all // KVH
    slice_cols = kv_weight.shape[1]
    quarters = HD // slice_cols
    scale = 1.0 / math.sqrt(HD)
    hadamard = jnp.asarray(hadamard_table(HB), jnp.float32)
    sign_row = (2 * signs - 1).astype(jnp.float32)
    stream = resid.reshape(rows_here, width).astype(jnp.float32)
    normed = (
        stream * lax.rsqrt(jnp.mean(stream * stream, axis=-1, keepdims=True) + norm_eps) * norm_gain
    )
    rotated = rotate_blocks(normed, sign_row, hadamard).astype(jnp.bfloat16)
    block_ids = jnp.arange(section_count, dtype=jnp.int32)
    offsets = jnp.cumsum(lengths) - lengths
    own_offset = jnp.sum(jnp.where(block_ids == section_here, offsets, 0))
    token_pos = (own_offset + jnp.arange(block_len, dtype=jnp.int32)).astype(jnp.float32)
    segment = lax.all_gather(rotated, "tensor", axis=0, tiled=True)
    projected = jnp.concatenate(
        [
            jnp.dot(segment, query_weight, preferred_element_type=jnp.float32),
            jnp.dot(segment, kv_weight, preferred_element_type=jnp.float32),
        ],
        axis=1,
    )
    query_cols = heads_here * HD
    local_queries = (
        rotary(projected[:, :query_cols].reshape(block_len, heads_here, HD), token_pos)
        .astype(jnp.bfloat16)
        .reshape(block_len, query_cols)
    )
    kv_slice = projected[:, query_cols:].astype(jnp.bfloat16)
    query_rows = lax.all_to_all(local_queries, "tensor", split_axis=0, concat_axis=1, tiled=True)
    query_tokens = tensor_here * rows_here + jnp.arange(rows_here, dtype=jnp.int32)
    carry_start = (
        jnp.full((KVH, group_size, rows_here), -1e30, jnp.float32),
        jnp.zeros((KVH, group_size, rows_here), jnp.float32),
        jnp.zeros((KVH, group_size, rows_here, HD), jnp.float32),
    )
    gathered = lax.all_gather(kv_slice[None], ("tensor", "section"), axis=0, tiled=True)
    split_cols = gathered.reshape(KVH, 2, quarters, section_count, block_len, slice_cols)
    all_pos = (offsets[:, None] + jnp.arange(block_len, dtype=jnp.int32)[None, :]).astype(
        jnp.float32
    )
    freq_full = jnp.concatenate([inverse_freqs(HD), inverse_freqs(HD)])
    angles = (
        (all_pos[..., None] * freq_full)
        .reshape(section_count, block_len, quarters, slice_cols)
        .transpose(2, 0, 1, 3)
    )
    raw_keys = split_cols[:, 0].astype(jnp.float32)
    turned = raw_keys * jnp.cos(angles) + swap_halves(raw_keys, quarters) * jnp.sin(angles)
    key_table = turned.astype(jnp.bfloat16).reshape(
        KVH, quarters, section_count * block_len, slice_cols
    )
    value_table = split_cols[:, 1].reshape(KVH, quarters, section_count * block_len, slice_cols)
    query_five = query_rows.reshape(rows_here, KVH, group_size, quarters, slice_cols)
    scores = (
        jnp.einsum("tkgqc,kqrc->kgtr", query_five, key_table, preferred_element_type=jnp.float32)
        * scale
    )
    key_index = jnp.arange(section_count * block_len, dtype=jnp.int32)
    key_block = key_index // block_len
    key_token = key_index % block_len
    key_length = jnp.sum(
        jnp.where(key_block[:, None] == block_ids[None, :], lengths[None, :], 0), axis=1
    )
    earlier = key_block < section_here
    same_block = (key_block == section_here)[None, :] & (
        key_token[None, :] <= query_tokens[:, None]
    )
    visible = (key_token < key_length)[None, :] & (earlier[None, :] | same_block)

    def combine_joint(rounded):
        return jnp.einsum(
            "kgtr,kqrc->kgtqc", rounded, value_table, preferred_element_type=jnp.float32
        ).reshape(KVH, group_size, rows_here, HD)

    row_max, row_total, running = absorb(carry_start, scores, visible, combine_joint)
    attended = (
        (running / row_total[..., None])
        .astype(jnp.bfloat16)
        .transpose(2, 0, 1, 3)
        .reshape(rows_here, heads_all * HD)
    )
    head_rows = lax.all_to_all(attended, "tensor", split_axis=1, concat_axis=0, tiled=True)
    branch = lax.psum_scatter(
        jnp.dot(head_rows, out_weight, preferred_element_type=jnp.float32).astype(jnp.bfloat16),
        "tensor",
        scatter_dimension=0,
        tiled=True,
    ).astype(jnp.float32)
    mixed = stream + unrotate_blocks(branch, sign_row, hadamard)
    return mixed.astype(jnp.bfloat16).reshape(1, rows_here, width)


def solution(mesh):
    return jax.shard_map(
        shards,
        mesh=mesh,
        in_specs=(
            P("section", "tensor", None),
            P(),
            P(),
            P(None, "tensor"),
            P(None, "tensor"),
            P("tensor", None),
            P(),
        ),
        out_specs=P("section", "tensor", None),
        check_vma=False,
    )
```

profile of v0, /device:TPU:192, one launch (start us, length us, event | category | flops | bytes accessed | tf_op | source)
XLA Modules:
  0.0 1055.6 jit_solution(9511898130928640143)
XLA Ops:
  6.6 1.1 convert_element_type.82
  7.6 1.1 multiply_reduce_fusion
  8.9 0.8 convert_bitcast_fusion
  9.7 1.4 fusion.22
  11.1 0.8 reshape.652
  12.0 192.7 %all-gather.7.cloned.1.call-done = bf16[32,12,8192]{2,1,0:T(8,128)(2,1)} async-done(((bf16[1,12,8192]{2,1,0:T(8,128)(2,1)}), bf16[32,12,8192]{2,1,0:T(8,128)(2,1)}) %all-gather.7.cloned.1.call-update) | async-done | bytes 6291472 | tf_op jit(solution)/shard_map/all_gather | solution.py:104
  204.7 8.8 reshape.653
  213.4 5.5 convolution_convert_fusion.1
  219.1 0.6 fusion.76
  220.0 0.7 add_convert_fusion.3
  220.9 0.8 multiply_cosine_fusion.1
  221.6 6.6 multiply_cosine_fusion
  228.2 6.4 fusion.94
  235.5 0.5 pad_maximum_fusion
  236.0 0.8 convert_element_type.98
  236.9 5.0 all-to-all-start
  242.0 9.3 all-to-all-done
  251.6 387.0 %all-gather.5.cloned.1.call-done = bf16[98304,64]{0,1:T(8,128)(2,1)} async-done(((bf16[384,64]{0,1:T(8,128)(2,1)}), bf16[98304,64]{0,1:T(8,128)(2,1)}) %all-gather.5.cloned.1.call-update) | async-done | bytes 12582928 | tf_op jit(solution)/shard_map/all_gather | solution.py:126
  638.5 7.4 copy.71
  645.9 11.8 %fusion.92 = (bf16[8,1,2,8,384,64]{4,3,2,1,0,5:T(8,128)(2,1)}, f32[8,2,8,384,64]{3,2,1,0,4:T(8,128)}, f32[8,1,2,8,384,64]{4,3,2,1,0,5:T(8,128)}) fusion(bf16[8,2,2,8,384,64]{4,3,2,1,0,5:T(8,128)(2,1)S(1)} %bitcast.102), kind=kLoop, calls=%fused_computation.170 | loop fusion | flops 3145728 | bytes 44040192 | tf_op jit(solution)/shard_map/slice | solution.py:142
  657.7 11.5 %slice_negate_fusion = (f32[8,1,8,384,64]{3,2,1,0,4:T(8,128)}, f32[8,1,8,384,64]{3,2,1,0,4:T(8,128)}) fusion(f32[8,2,8,384,64]{3,2,1,0,4:T(8,128)} %get-tuple-element.8), kind=kLoop, calls=%fused_computation.17 | loop fusion | flops 1572864 | bytes 25165824 | tf_op jit(solution)/shard_map/neg | solution.py:66
  669.2 7.2 reshape.661
  676.4 9.2 copy.63
  685.6 7.2 reshape.662
  692.7 9.1 copy.64
  701.8 16.2 %reshape.660 = f32[8,2,3072,64]{2,1,0,3:T(2,128)} reshape(f32[8,1,2,8,384,64]{4,3,2,1,0,5:T(8,128)} %get-tuple-element.9) | data formatting | bytes 25165824 | tf_op jit(solution)/shard_map/convert_element_type | solution.py:137
  718.0 20.2 %fusion.3 = (f32[8,8,12]{2,1,0:T(8,128)S(1)}, f32[8,3072,12,8,1]{1,2,4,3,0:T(8,128)}) fusion(pred[12,3072]{1,0:T(8,128)(4,1)S(1)} %or_and_fusion, bf16[12,8,8,2,64]{4,3,2,1,0:T(2,128)(2,1)S(1)} %reshape.643, f32[8,1,3072,64]{2,3,1,0:T(8,128)} %copy.64, f32[8,1,3072,64]{2,3,1,0:T(8,128)} %copy.63, f32[8,2,3072,64]{2,1,0,3:T(2,128)} %reshape.660, ...), kind=kOutput, calls=%fused_computation.5 | convolution fusion | flops 626785536 | bytes 37985280 | tf_op jit(solution)/shard_map/tkgqc,kqrc->kgtr/dot_general | solution.py:145
  738.2 7.8 fusion.6
  746.1 13.0 %reshape.663 = bf16[8,2,3072,64]{2,1,0,3:T(2,128)(2,1)} reshape(bf16[8,1,2,8,384,64]{4,3,2,1,0,5:T(8,128)(2,1)} %get-tuple-element.7) | data formatting | bytes 12582912 | tf_op jit(solution)/shard_map/reshape;squeeze | solution.py:142
  759.1 19.8 %fusion.9 = f32[8,8,12,2,64]{4,2,3,1,0:T(8,128)S(1)} fusion(f32[8,3072,12,8,1]{1,2,4,3,0:T(8,128)} %get-tuple-element.21, bf16[8,2,3072,64,1]{2,1,0,3,4:T(2,128)(2,1)} %bitcast.104, f32[8,8,12]{2,1,0:T(8,128)S(1)} %broadcast_maximum_fusion, pred[12,3072]{1,0:T(8,128)(4,1)S(1)} %or_and_fusion), kind=kOutput, calls=%fused_computation.14 | convolution fusion | flops 613416960 | bytes 16161792 | tf_op jit(solution)/shard_map/kgtr,kqrc->kgtqc/dot_general | solution.py:161
  780.2 12.4 %all_to_all.32 = bf16[12,32,256]{2,0,1:T(8,128)(2,1)S(1)} all-to-all(bf16[12,32,256]{2,0,1:T(8,128)(2,1)S(1)} %copy.57), channel_id=1, replica_groups=mesh['tensor'=32,'section'=8] {'tensor'}, dimensions={1} | all-to-all | bytes 393216 | tf_op jit(solution)/shard_map/all_to_all | solution.py:172
  792.7 6.8 convolution_convert_fusion
  799.4 182.5 %fusion = bf16[16,8192]{1,0:T(8,128)(2,1)S(1)} fusion(bf16[384,8192]{1,0:T(8,128)(2,1)} %convolution_convert_fusion), kind=kCustom, calls=%all-reduce-scatter | all-reduce-scatter fusion | flops 4194305 | bytes 6554624
  981.9 2.0 collective-permute-start
  984.0 1.3 collective-permute-start.1
  985.4 1.3 collective-permute-start.7
  986.7 2.5 collective-permute-start.2
  989.2 7.7 collective-permute-start.3
  997.0 10.3 collective-permute-done.7
  1007.3 1.3 collective-permute-start.4
  1008.7 1.3 collective-permute-start.5
  1010.0 8.5 collective-permute-start.6
  1018.5 0.7 dynamic-slice.4
  1019.9 0.6 copy-done.6
  1020.7 0.7 copy-done.9
  1021.7 24.4 %concatenate.20 = bf16[140,8192]{1,0:T(8,128)(2,1)S(1)} concatenate(bf16[12,8192]{1,0:T(8,128)(2,1)} %copy-done.5, bf16[16,8192]{1,0:T(8,128)(2,1)} %collective-permute-done.6, bf16[16,8192]{1,0:T(8,128)(2,1)} %copy-done.9, bf16[16,8192]{1,0:T(8,128)(2,1)} %copy-done.8, bf16[16,8192]{1,0:T(8,128)(2,1)} %copy-done.7, bf16[16,8192]{1,0:T(8,128)(2,1)} %copy-done.6, ...), dimensions={0} | concatenate | bytes 4587520
  1046.2 0.5 fusion.27
  1046.8 1.7 add_convert_fusion
  (74 shorter events, 4.1 us)
Async XLA Ops:
  6.5 206.9 %copy-start = (bf16[8192,64]{0,1:T(8,128)(2,1)S(1)}, bf16[8192,64]{0,1:T(8,128)(2,1)}, u32[]{:S(2)}) copy-start(bf16[8192,64]{0,1:T(8,128)(2,1)} %param.11) | copy-start | bytes 3145732
  6.5 198.1 %all-gather.7.cloned.1.call-start = ((), (), s32[]{:S(2)}) async-start(), calls=%async_computation.3 | async-start | bytes 8650752 | tf_op jit(solution)/shard_map/all_gather | solution.py:104
  11.9 626.6 %all-gather.5.cloned.1.call-start = ((), (), s32[]{:S(2)}) async-start(), calls=%async_computation.2 | async-start | bytes 12632064 | tf_op jit(solution)/shard_map/all_gather | solution.py:126
  213.4 5.5 copy-start.11
  236.9 14.4 %all-to-all-start = ((bf16[32,12,256]{2,1,0:T(8,128)(2,1)}), bf16[32,12,256]{2,1,0:T(8,128)(2,1)S(1)}, u32[]{:S(2)}, u32[]{:S(2)}) async-start(bf16[32,12,256]{2,1,0:T(8,128)(2,1)} %convert_element_type.98), calls=%async_computation | async-start | bytes 524288 | tf_op jit(solution)/shard_map/all_to_all | solution.py:119
  792.6 225.9 %copy-start.12 = (u32[256]{0:T(256)S(1)}, u32[256]{0:T(256)}, u32[]{:S(2)}) copy-start(u32[256]{0:T(256)} %constant.227) | copy-start | bytes 3076
  792.7 227.2 %copy-start.10 = (s32[8192]{0:T(1024)S(1)}, s32[8192]{0:T(1024)}, u32[]{:S(2)}) copy-start(s32[8192]{0:T(1024)} %param.9) | copy-start | bytes 98308
  792.7 255.9 %copy-start.1 = (bf16[8192,64]{0,1:T(8,128)(2,1)S(1)}, bf16[8192,64]{0,1:T(8,128)(2,1)}, u32[]{:S(2)}) copy-start(bf16[8192,64]{0,1:T(8,128)(2,1)} %param.11) | copy-start | bytes 3145732
  981.9 38.0 %copy-start.2 = (bf16[16,8192]{1,0:T(8,128)(2,1)}, bf16[16,8192]{1,0:T(8,128)(2,1)S(1)}, u32[]{:S(2)}) copy-start(bf16[16,8192]{1,0:T(8,128)(2,1)S(1)} %fusion) | copy-start | bytes 786436
  981.9 26.7 %collective-permute-start = (bf16[16,8192]{1,0:T(8,128)(2,1)S(1)}, bf16[16,8192]{1,0:T(8,128)(2,1)S(1)}, u32[]{:S(2)}, u32[]{:S(2)}) collective-permute-start(bf16[16,8192]{1,0:T(8,128)(2,1)S(1)} %fusion), channel_id=1, source_target_pairs={{0,8},{8,16},{16,24},{24,32},{32,40},{40,48},{48,56},{56,64},{64,7... | collective-permute-start | bytes 786440
  984.0 26.0 %collective-permute-start.1 = (bf16[16,8192]{1,0:T(8,128)(2,1)S(1)}, bf16[16,8192]{1,0:T(8,128)(2,1)S(1)}, u32[]{:S(2)}, u32[]{:S(2)}) collective-permute-start(bf16[16,8192]{1,0:T(8,128)(2,1)S(1)} %fusion), channel_id=1, source_target_pairs={{0,16},{8,24},{16,32},{24,40},{32,48},{40,56},{48,64},{56,72},{64,... | collective-permute-start | bytes 786440
  985.4 22.0 %collective-permute-start.7 = (bf16[12,8192]{1,0:T(8,128)(2,1)S(1)}, bf16[12,8192]{1,0:T(8,128)(2,1)S(1)}, u32[]{:S(2)}, u32[]{:S(2)}) collective-permute-start(bf16[12,8192]{1,0:T(8,128)(2,1)S(1)} %slice.30), channel_id=1, source_target_pairs={{0,64},{8,72},{16,80},{24,88},{32,96},{40,104},{48,112},{56,120},{... | collective-permute-start | bytes 589832
  986.7 33.2 %collective-permute-start.2 = (bf16[16,8192]{1,0:T(8,128)(2,1)S(1)}, bf16[16,8192]{1,0:T(8,128)(2,1)S(1)}, u32[]{:S(2)}, u32[]{:S(2)}) collective-permute-start(bf16[16,8192]{1,0:T(8,128)(2,1)S(1)} %fusion), channel_id=1, source_target_pairs={{0,24},{8,32},{16,40},{24,48},{32,56},{40,64},{48,72},{56,80},{64,... | collective-permute-start | bytes 786440
  989.2 30.7 %collective-permute-start.3 = (bf16[16,8192]{1,0:T(8,128)(2,1)S(1)}, bf16[16,8192]{1,0:T(8,128)(2,1)S(1)}, u32[]{:S(2)}, u32[]{:S(2)}) collective-permute-start(bf16[16,8192]{1,0:T(8,128)(2,1)S(1)} %fusion), channel_id=1, source_target_pairs={{0,32},{8,40},{16,48},{24,56},{32,64},{40,72},{48,80},{56,88},{64,... | collective-permute-start | bytes 786440
  1007.3 11.2 %copy-start.5 = (bf16[12,8192]{1,0:T(8,128)(2,1)}, bf16[12,8192]{1,0:T(8,128)(2,1)S(1)}, u32[]{:S(2)}) copy-start(bf16[12,8192]{1,0:T(8,128)(2,1)S(1)} %collective-permute-done.7) | copy-start | bytes 589828
  1007.3 12.6 %collective-permute-start.4 = (bf16[16,8192]{1,0:T(8,128)(2,1)S(1)}, bf16[16,8192]{1,0:T(8,128)(2,1)S(1)}, u32[]{:S(2)}, u32[]{:S(2)}) collective-permute-start(bf16[16,8192]{1,0:T(8,128)(2,1)S(1)} %fusion), channel_id=1, source_target_pairs={{0,40},{8,48},{16,56},{24,64},{32,72},{40,80},{48,88},{56,96},{64,... | collective-permute-start | bytes 786440
  1008.6 1.3 copy-start.3
  1008.7 11.3 %collective-permute-start.5 = (bf16[16,8192]{1,0:T(8,128)(2,1)S(1)}, bf16[16,8192]{1,0:T(8,128)(2,1)S(1)}, u32[]{:S(2)}, u32[]{:S(2)}) collective-permute-start(bf16[16,8192]{1,0:T(8,128)(2,1)S(1)} %fusion), channel_id=1, source_target_pairs={{0,48},{8,56},{16,64},{24,72},{32,80},{40,88},{48,96},{56,104},{64... | collective-permute-start | bytes 786440
  1010.0 8.5 copy-start.4
  1010.0 11.7 %collective-permute-start.6 = (bf16[16,8192]{1,0:T(8,128)(2,1)S(1)}, bf16[16,8192]{1,0:T(8,128)(2,1)}, u32[]{:S(2)}, u32[]{:S(2)}) collective-permute-start(bf16[16,8192]{1,0:T(8,128)(2,1)S(1)} %fusion), channel_id=1, source_target_pairs={{0,56},{8,64},{16,72},{24,80},{32,88},{40,96},{48,104},{56,112},{6... | collective-permute-start | bytes 786440
  1019.9 0.7 copy-start.6
  1019.9 0.8 copy-start.7
  1019.9 0.8 copy-start.8
  1020.7 0.7 copy-start.9
Sparse Core Ops, SparseCore 0:
  12.1 192.5 all-gather.6
  219.1 419.4 all-gather.4
where the time goes:
time: 1080 us; the launch traced here: 1060 us
  waiting for transfers between devices  600 us (56%)
  blocking collectives  195 us (18%)
  local copies, waits for them, and re-layouts  108 us (10%)
  matrix products  60.5 us (6%)
  other arithmetic  46.2 us (4%)
  starting transfers between devices  31.1 us (3%)
  between operations  14.7 us (1%)
    all_gather x1, waiting for transfers between devices, shards(): lax.all_gather(kv_slice[None], ('tensor', 'section'), axis=0, tiled=True)  387 us
    all_gather x1, waiting for transfers between devices, shards(): segment = lax.all_gather(rotated, 'tensor', axis=0, tiled=True)  193 us
    unnamed x1, blocking collectives  182 us
    unnamed x37, local copies, waits for them, and re-layouts  44.3 us
    concatenate x4, local copies, waits for them, and re-layouts, swap_halves(): return jnp.concatenate([-inputs[:, middle:], inputs[:, :middle]], axis=1)  32.6 us
    unnamed x8, starting transfers between devices  26.1 us
  transfers between devices with their start and end apart: 11, of which 5 were waited for; matrix products, arithmetic and copies ran while one was open for 2% of the time, Pallas kernels for 0%

commit v1 on v0

v1 whole, which is shorter than its diff:
```python
import functools
import math

import jax
import jax.numpy as jnp
import numpy as np
from jax import lax
from jax.experimental import pallas as pl
from jax.experimental.pallas import tpu as pltpu
from jax.sharding import PartitionSpec as P

MESH = pl.DeviceIdType.MESH
D = 8192
HD = 128
HB = 128
ROWS = 12
TOK = 384
BLOCKS = 8
NC = 4
CW = D // NC
SUB = 4
SW = CW // SUB
PR = SUB * ROWS
QC = 256
KC = 64
rope_base = 500000.0
norm_eps = 1e-05
NEG = -1e30


def hadamard(extent):
    index = np.arange(extent)
    bits = index[:, None] & index[None, :]
    parity = np.zeros((extent, extent), np.int64)
    while bits.any():
        parity += bits & 1
        bits = bits >> 1
    return (1 - 2 * (parity % 2)).astype(np.float32)


def token_order():
    order = []
    for half in range(2):
        for j in range(4):
            for i in range(4):
                y, x = (j, i) if half == 0 else (i, j)
                t = (y * 4 + x) * 2 + half
                order.extend(range(t * ROWS, (t + 1) * ROWS))
    return np.array(order)


def here():
    t = lax.axis_index("tensor")
    s = lax.axis_index("section")
    y = t // 8
    x = lax.rem(t // 2, 4)
    z = (s // 2) * 2 + lax.rem(t, 2)
    return y, x, z, lax.rem(s, 2)


def device(y, x, z, c):
    return ((y * 4 + x) * 2 + lax.rem(z, 2), (z // 2) * 2 + c)


def shift(value, by, size):
    return lax.rem(value + (by + size), size)


def split3(value):
    high = value.astype(jnp.bfloat16)
    rest = value - high.astype(jnp.float32)
    middle = rest.astype(jnp.bfloat16)
    low = (rest - middle.astype(jnp.float32)).astype(jnp.bfloat16)
    return jnp.concatenate([high, middle, low], axis=1)


def greet(partners):
    barrier = pltpu.get_barrier_semaphore()
    for partner in partners:
        pl.semaphore_signal(barrier, inc=1, device_id=partner, device_id_type=MESH)
    pl.semaphore_wait(barrier, len(partners))


def remote(src, dst, send, recv, target):
    return pltpu.make_async_remote_copy(
        src_ref=src,
        dst_ref=dst,
        send_sem=send,
        recv_sem=recv,
        device_id=target,
        device_id_type=MESH,
    )


def project_kernel(
    resid, gain_sign, had, q_hbm, kv_hbm, cos_ref, sin_ref, q_out, kv_out,
    wq, wkv, p2, blocks, acc_q, acc_kv, w_sem, sz, rz, s2, r2, s3, r3,
):
    y, x, z, core = here()
    low = lax.rem(z, 2)
    mate = z + 1 - 2 * low

    def inner(h, by):
        return device(shift(y, by * h, 4), shift(x, by * (1 - h), 4), z, core)

    def outer(h, by):
        return device(shift(y, by * (1 - h), 4), shift(x, by * h, 4), z, core)

    def inner_pos(h):
        return x * (1 - h) + y * h

    def outer_pos(h):
        return y * (1 - h) + x * h

    greet(
        [device(y, x, mate, core)]
        + [inner(h, by) for h in range(2) for by in (1, -1)]
    )
    loads = [
        pltpu.make_async_copy(q_hbm, wq, w_sem.at[0]),
        pltpu.make_async_copy(kv_hbm, wkv, w_sem.at[1]),
    ]
    for load in loads:
        load.start()

    stream = resid[0].astype(jnp.float32)
    normed = (
        stream
        * lax.rsqrt(jnp.mean(stream * stream, axis=-1, keepdims=True) + norm_eps)
        * gain_sign[...]
    )
    stacked = []
    for c in range(NC):
        for b in range(SW // HB):
            stacked.append(
                jnp.concatenate(
                    [
                        normed[:, c * CW + j * SW + b * HB : c * CW + j * SW + (b + 1) * HB]
                        for j in range(SUB)
                    ],
                    axis=0,
                )
            )
    stacked = jnp.concatenate(stacked, axis=0)
    rotated = jnp.dot(split3(stacked), had[...], preferred_element_type=jnp.float32) * (
        1.0 / math.sqrt(HB)
    )
    own_pos = inner_pos(low)
    for c in range(NC):
        parts = [
            rotated[(c * (SW // HB) + b) * PR : (c * (SW // HB) + b + 1) * PR]
            for b in range(SW // HB)
        ]
        p2[low, own_pos, c] = jnp.concatenate(parts, axis=1).astype(jnp.bfloat16)

    started = []

    def go(copy):
        copy.start()
        started.append(copy)

    def z_copy(c, half):
        ref = p2.at[half, inner_pos(half), c]
        return remote(ref, ref, sz.at[c], rz.at[c], device(y, x, mate, core))

    def direct2(h, c):
        ref = p2.at[h, inner_pos(h), c]
        go(remote(ref, ref, s2.at[h, 0, c], r2.at[h, 0, c], inner(h, 1)))
        go(remote(ref, ref, s2.at[h, 1, c], r2.at[h, 1, c], inner(h, -1)))

    def direct3(h, c):
        ref = blocks.at[h, outer_pos(h), c]
        go(remote(ref, ref, s3.at[h, 0, c], r3.at[h, 0, c], outer(h, 1)))
        go(remote(ref, ref, s3.at[h, 1, c], r3.at[h, 1, c], outer(h, -1)))

    def arrive(buf, pos, ssem, rsem, peer, h, c):
        for kind, by in ((0, -1), (1, 1)):
            ref = buf.at[h, shift(pos(h), by, 4), c]
            remote(ref, ref, ssem.at[h, kind, c], rsem.at[h, kind, c], peer(h, 1)).wait_recv()
        by = -1 if c % 2 == 0 else 1
        ref = buf.at[h, shift(pos(h), by, 4), c]
        go(remote(ref, ref, ssem.at[h, 2, c], rsem.at[h, 2, c], peer(h, -by)))

    def last(buf, pos, ssem, rsem, peer, h, c):
        ref = buf.at[h, shift(pos(h), 2, 4), c]
        remote(ref, ref, ssem.at[h, 2, c], rsem.at[h, 2, c], peer(h, 1)).wait_recv()

    for c in range(NC):
        go(z_copy(c, low))
        direct2(low, c)
    for c in range(NC):
        z_copy(c, 1 - low).wait_recv()
        direct2(1 - low, c)
    for c in range(NC + 1):
        if c < NC:
            for h in range(2):
                arrive(p2, inner_pos, s2, r2, inner, h, c)
        if c > 0:
            for h in range(2):
                last(p2, inner_pos, s2, r2, inner, h, c - 1)
                pieces = [p2[h, i, c - 1].astype(jnp.float32) for i in range(4)]
                joined = jnp.concatenate(
                    [
                        jnp.concatenate(
                            [piece[j * ROWS : (j + 1) * ROWS] for piece in pieces], axis=0
                        )
                        for j in range(SUB)
                    ],
                    axis=1,
                )
                blocks[h, outer_pos(h), c - 1] = joined.astype(jnp.bfloat16)
                direct3(h, c - 1)
    for load in loads:
        load.wait()
    for c in range(NC + 1):
        if c < NC:
            for h in range(2):
                arrive(blocks, outer_pos, s3, r3, outer, h, c)
        if c > 0:
            for h in range(2):
                last(blocks, outer_pos, s3, r3, outer, h, c - 1)
            left = blocks[:, :, c - 1].reshape(TOK, CW)
            rows = pl.ds((c - 1) * CW, CW)
            part_q = jnp.dot(left, wq[rows], preferred_element_type=jnp.float32)
            part_kv = jnp.dot(left, wkv[rows], preferred_element_type=jnp.float32)
            if c == 1:
                acc_q[...] = part_q
                acc_kv[...] = part_kv
            else:
                acc_q[...] += part_q
                acc_kv[...] += part_kv
    kv_out[...] = jnp.transpose(acc_kv[...]).astype(jnp.bfloat16)
    turned = jnp.transpose(acc_q[...])
    cosine, sine = cos_ref[...], sin_ref[...]
    half = HD // 2
    for head in range(2):
        first = turned[head * HD : head * HD + half]
        second = turned[head * HD + half : (head + 1) * HD]
        q_out[head * HD : head * HD + half] = (first * cosine - second * sine).astype(jnp.bfloat16)
        q_out[head * HD + half : (head + 1) * HD] = (second * cosine + first * sine).astype(
            jnp.bfloat16
        )
    for copy in started:
        copy.wait_send()


def attend_kernel(
    lengths, q_ref, kv_ref, off_cos, off_sin, tok_cos, tok_sin, key_tok, query_tok,
    out_hbm, resid, sign_row, had, mixed,
    wo, kvs, att, parts, raw1, fin1, parts2, raw2, fin2, sums, sums_bf, last_z, acc,
    w_sem, sx, rx, skv, rkv, sc, rc, s1, r1, s2, r2, sz, rz,
):
    y, x, z, core = here()
    low = lax.rem(z, 2)
    mate = z + 1 - 2 * low
    section = lax.axis_index("section")

    def inner(h, by):
        return device(shift(y, by * (1 - h), 4), shift(x, by * h, 4), z, core)

    def outer(h, by):
        return device(shift(y, by * h, 4), shift(x, by * (1 - h), 4), z, core)

    def inner_pos(h):
        return y * (1 - h) + x * h

    def outer_pos(h):
        return x * (1 - h) + y * h

    def along(by):
        return device(y, x, shift(z, by, 8), core)

    other_core = device(y, x, z, 1 - core)
    own_x = lax.rem(x, 2)
    x_mate = device(y, x + 1 - 2 * own_x, z, core)
    greet([along(1), along(-1), other_core] + [inner(h, by) for h in range(2) for by in (1, -1)])
    load = pltpu.make_async_copy(out_hbm, wo, w_sem)
    load.start()
    started = []

    def go(copy):
        copy.start()
        started.append(copy)

    def side(e):
        return own_x if e == 0 else 1 - own_x

    def hop(e, src_by, kind, dist, target):
        ref = kvs.at[core, side(e), shift(z, src_by, 8)]
        return remote(ref, ref, skv.at[kind, dist, e], rkv.at[kind, dist, e], target)

    def to_core(e, src_by):
        k = src_by % 8
        ref = kvs.at[core, side(e), shift(z, src_by, 8)]
        go(remote(ref, ref, sc.at[e, k], rc.at[e, k], other_core))

    kvs[core, own_x, z] = kv_ref[...]
    own = kvs.at[core, own_x, z]
    go(remote(own, own, sx, rx, x_mate))
    go(hop(0, 0, 0, 0, along(1)))
    go(hop(0, 0, 1, 0, along(-1)))
    to_core(0, 0)
    theirs = kvs.at[core, 1 - own_x, z]
    remote(theirs, theirs, sx, rx, x_mate).wait_recv()
    go(hop(1, 0, 0, 0, along(1)))
    go(hop(1, 0, 1, 0, along(-1)))
    to_core(1, 0)
    for dist in range(4):
        for e in range(2):
            for kind, sgn in ((0, -1), (1, 1)):
                if dist == 3 and kind != e:
                    continue
                by = sgn * (dist + 1)
                hop(e, by, kind, dist, along(1)).wait_recv()
                if dist < 2 or (dist == 2 and kind == e):
                    go(hop(e, by, kind, dist + 1, along(-sgn)))
                to_core(e, by)
    for e in range(2):
        for k in range(8):
            ref = kvs.at[1 - core, side(e), shift(z, k, 8)]
            remote(ref, ref, sc.at[e, k], rc.at[e, k], other_core).wait_recv()

    scale = math.log2(math.e) / math.sqrt(HD)
    half = HD // 2

    def block(index):
        c = lax.rem(index, 2)
        pair = pl.ds((index // 2) * 2, 2)
        raw = kvs[c, 0, pair].astype(jnp.float32)
        value = kvs[c, 1, pair].reshape(HD, TOK)
        oc, os = off_cos[index], off_sin[index]
        cosine = oc * tok_cos[...] - os * tok_sin[...]
        sine = os * tok_cos[...] + oc * tok_sin[...]
        first, second = raw[0], raw[1]
        key = jnp.concatenate(
            [first * cosine - second * sine, second * cosine + first * sine], axis=0
        )
        key = jnp.transpose(key).astype(jnp.bfloat16)
        query = q_ref[...]
        scores = jnp.concatenate(
            [
                jnp.dot(key, query[:HD], preferred_element_type=jnp.float32),
                jnp.dot(key, query[HD:], preferred_element_type=jnp.float32),
            ],
            axis=1,
        )
        return scores, value

    scores, value = block(section)
    seen = (key_tok[...] < lengths[section]) & (key_tok[...] <= query_tok[...])
    scores = jnp.where(seen, scores, NEG)
    top = jnp.max(scores, axis=0, keepdims=True)
    weights = jnp.where(seen, jnp.exp2((scores - top) * scale), 0.0)
    total = jnp.sum(weights, axis=0, keepdims=True)
    acc[...] = jnp.dot(value, weights.astype(jnp.bfloat16), preferred_element_type=jnp.float32)

    def step(index, carry):
        top, total = carry
        scores, value = block(index)
        scores = scores + jnp.where(key_tok[...] < lengths[index], 0.0, NEG)
        new_top = jnp.maximum(top, jnp.max(scores, axis=0, keepdims=True))
        weights = jnp.exp2((scores - new_top) * scale)
        fade = jnp.exp2((top - new_top) * scale)
        acc[...] = acc[...] * fade + jnp.dot(
            value, weights.astype(jnp.bfloat16), preferred_element_type=jnp.float32
        )
        return new_top, total * fade + jnp.sum(weights, axis=0, keepdims=True)

    top, total = lax.fori_loop(0, section, step, (top, total))
    attended = acc[...] / total
    for head in range(2):
        att[:, head * HD : (head + 1) * HD] = jnp.transpose(
            attended[:, head * TOK : (head + 1) * TOK]
        ).astype(jnp.bfloat16)

    def send_raw(buf, raw, pos, ssem, rsem, peer, h, c):
        by = 1 if c % 2 == 0 else -1
        go(
            remote(
                buf.at[h, shift(pos(h), 2, 4), c], raw.at[h, c], ssem.at[h, 2, c],
                rsem.at[h, 2, c], peer(h, by),
            )
        )

    def send_fin(buf, fin, pos, ssem, rsem, peer, h, c, kind):
        by = 1 if kind == 0 else -1
        go(
            remote(
                buf.at[h, shift(pos(h), by, 4), c], fin.at[h, kind, c], ssem.at[h, kind, c],
                rsem.at[h, kind, c], peer(h, by),
            )
        )

    def pass_on(buf, raw, fin, pos, ssem, rsem, peer, h, c):
        kind, by = (0, 1) if c % 2 == 0 else (1, -1)
        ref = raw.at[h, c]
        remote(ref, ref, ssem.at[h, 2, c], rsem.at[h, 2, c], peer(h, 1)).wait_recv()
        slot = shift(pos(h), by, 4)
        buf[h, slot, c] = (
            buf[h, slot, c].astype(jnp.float32) + raw[h, c].astype(jnp.float32)
        ).astype(jnp.bfloat16)
        send_fin(buf, fin, pos, ssem, rsem, peer, h, c, kind)

    def finish(buf, fin, pos, ssem, rsem, peer, h, c):
        for kind in range(2):
            ref = fin.at[h, kind, c]
            remote(ref, ref, ssem.at[h, kind, c], rsem.at[h, kind, c], peer(h, 1)).wait_recv()
        return (
            buf[h, pos(h), c].astype(jnp.float32)
            + fin[h, 0, c].astype(jnp.float32)
            + fin[h, 1, c].astype(jnp.float32)
        )

    ring1 = (inner_pos, s1, r1, inner)
    ring2 = (outer_pos, s2, r2, outer)
    load.wait()
    for c in range(NC):
        partial = jnp.dot(
            att[...], wo[:, c * CW : (c + 1) * CW], preferred_element_type=jnp.float32
        ).astype(jnp.bfloat16)
        parts[:, :, c] = partial.reshape(2, 4, PR, CW)
        for h in range(2):
            send_raw(parts, raw1, *ring1, h, c)
            send_fin(parts, fin1, *ring1, h, c, 1 if c % 2 == 0 else 0)
    for c in range(NC):
        for h in range(2):
            pass_on(parts, raw1, fin1, *ring1, h, c)

    def z_copy(c, half):
        return remote(
            sums_bf.at[half, c], last_z.at[c], sz.at[c], rz.at[c], device(y, x, mate, core)
        )

    for c in range(NC + 2):
        if c < NC:
            for h in range(2):
                done = finish(parts, fin1, *ring1, h, c)
                for i in range(4):
                    parts2[h, i, c] = jnp.concatenate(
                        [
                            done[i * ROWS : (i + 1) * ROWS, j * SW : (j + 1) * SW]
                            for j in range(SUB)
                        ],
                        axis=0,
                    ).astype(jnp.bfloat16)
                send_raw(parts2, raw2, *ring2, h, c)
                send_fin(parts2, fin2, *ring2, h, c, 1 if c % 2 == 0 else 0)
        if 0 < c <= NC:
            for h in range(2):
                pass_on(parts2, raw2, fin2, *ring2, h, c - 1)
        if c > 1:
            for h in range(2):
                done = finish(parts2, fin2, *ring2, h, c - 2)
                sums[h, c - 2] = done
                sums_bf[h, c - 2] = done.astype(jnp.bfloat16)
            go(z_copy(c - 2, 1 - low))
    stacked = []
    for c in range(NC):
        z_copy(c, low).wait_recv()
        branch = sums[low, c] + last_z[c].astype(jnp.float32)
        stacked += [branch[:, b * HB : (b + 1) * HB] for b in range(SW // HB)]
    stacked = jnp.concatenate(stacked, axis=0)
    back = jnp.dot(split3(stacked), had[...], preferred_element_type=jnp.float32) * (
        1.0 / math.sqrt(HB)
    )
    columns = []
    for c in range(NC):
        for j in range(SUB):
            for b in range(SW // HB):
                row = (c * (SW // HB) + b) * PR + j * ROWS
                columns.append(back[row : row + ROWS])
    back = jnp.concatenate(columns, axis=1)
    mixed[0] = (resid[0].astype(jnp.float32) + sign_row[...] * back).astype(jnp.bfloat16)
    for copy in started:
        copy.wait_send()


def vmem(shape, dtype):
    return pltpu.VMEM(shape, dtype)


def shards(resid, norm_gain, signs, query_weight, kv_weight, out_weight, lengths):
    bf16, f32 = jnp.bfloat16, jnp.float32
    dma = pltpu.SemaphoreType.DMA
    in_vmem = pl.BlockSpec(memory_space=pltpu.VMEM)
    in_any = pl.BlockSpec(memory_space=pl.ANY)
    order = token_order()
    inverse = np.exp(np.arange(HD // 2) * (-2.0 * math.log(rope_base) / HD))
    angles = inverse[:, None] * order[None, :]
    tok_cos = jnp.asarray(np.cos(angles), f32)
    tok_sin = jnp.asarray(np.sin(angles), f32)
    offsets = (jnp.cumsum(lengths) - lengths).astype(f32)
    off_angles = offsets[:, None] * jnp.asarray(inverse, f32)[None, :]
    off_cos = jnp.cos(off_angles)[:, :, None]
    off_sin = jnp.sin(off_angles)[:, :, None]
    here_section = lax.axis_index("section")
    oc = lax.dynamic_index_in_dim(off_cos, here_section, 0, keepdims=False)
    os = lax.dynamic_index_in_dim(off_sin, here_section, 0, keepdims=False)
    cosine = oc * tok_cos - os * tok_sin
    sine = os * tok_cos + oc * tok_sin
    had = hadamard(HB)
    had3 = jnp.asarray(np.concatenate([had, had, had], axis=0), bf16)
    sign_row = (2 * signs - 1).astype(f32)[None, :]
    gain_sign = norm_gain[None, :] * sign_row

    queries, kv = pl.pallas_call(
        project_kernel,
        out_shape=(
            jax.ShapeDtypeStruct((QC, TOK), bf16),
            jax.ShapeDtypeStruct((KC, TOK), bf16),
        ),
        in_specs=[in_vmem, in_vmem, in_vmem, in_any, in_any, in_vmem, in_vmem],
        out_specs=(in_vmem, in_vmem),
        scratch_shapes=[
            vmem((D, QC), bf16),
            vmem((D, KC), bf16),
            vmem((2, 4, NC, PR, SW), bf16),
            vmem((2, 4, NC, PR, CW), bf16),
            vmem((TOK, QC), f32),
            vmem((TOK, KC), f32),
            dma((2,)),
            dma((NC,)),
            dma((NC,)),
            dma((2, 3, NC)),
            dma((2, 3, NC)),
            dma((2, 3, NC)),
            dma((2, 3, NC)),
        ],
        compiler_params=pltpu.CompilerParams(
            collective_id=1, has_side_effects=True, vmem_limit_bytes=40 << 20
        ),
        name="project",
    )(resid, gain_sign, had3, query_weight, kv_weight, cosine, sine)

    key_tok = jnp.asarray(order[:, None], jnp.int32)
    query_tok = jnp.asarray(np.concatenate([order, order])[None, :], jnp.int32)
    return pl.pallas_call(
        attend_kernel,
        out_shape=jax.ShapeDtypeStruct(resid.shape, bf16),
        in_specs=[pl.BlockSpec(memory_space=pltpu.SMEM)]
        + [in_vmem] * 8
        + [in_any]
        + [in_vmem] * 3,
        out_specs=in_vmem,
        scratch_shapes=[
            vmem((QC, D), bf16),
            vmem((2, 2, 8, KC, TOK), bf16),
            vmem((TOK, QC), bf16),
            vmem((2, 4, NC, PR, CW), bf16),
            vmem((2, NC, PR, CW), bf16),
            vmem((2, 2, NC, PR, CW), bf16),
            vmem((2, 4, NC, PR, SW), bf16),
            vmem((2, NC, PR, SW), bf16),
            vmem((2, 2, NC, PR, SW), bf16),
            vmem((2, NC, PR, SW), f32),
            vmem((2, NC, PR, SW), bf16),
            vmem((NC, PR, SW), bf16),
            vmem((HD, 2 * TOK), f32),
            dma,
            dma,
            dma,
            dma((2, 4, 2)),
            dma((2, 4, 2)),
            dma((2, 8)),
            dma((2, 8)),
            dma((2, 3, NC)),
            dma((2, 3, NC)),
            dma((2, 3, NC)),
            dma((2, 3, NC)),
            dma((NC,)),
            dma((NC,)),
        ],
        compiler_params=pltpu.CompilerParams(
            collective_id=2, has_side_effects=True, vmem_limit_bytes=50 << 20
        ),
        name="attend",
    )(
        lengths, queries, kv, off_cos, off_sin, tok_cos, tok_sin, key_tok, query_tok,
        out_weight, resid, sign_row, had3,
    )


def solution(mesh):
    return jax.shard_map(
        shards,
        mesh=mesh,
        in_specs=(
            P("section", "tensor", None),
            P(),
            P(),
            P(None, "tensor"),
            P(None, "tensor"),
            P("tensor", None),
            P(),
        ),
        out_specs=P("section", "tensor", None),
        check_vma=False,
    )
```

time: 1080 us -> 131 us (0.12); the launches traced: 1060 us -> 130 us
  waiting for transfers between devices: 600 us -> 0 us
  blocking collectives: 195 us -> 0 us
  Pallas kernels: 0 us -> 118 us
  local copies, waits for them, and re-layouts: 108 us -> 6.95 us
  matrix products: 60.5 us -> 0 us
  other arithmetic: 46.2 us -> 5.1 us
  starting transfers between devices: 31.1 us -> 0 us
  between operations: 14.7 us -> 0.21 us
    all_gather x2 -> x0, waiting for transfers between devices: 580 us -> none  [the longest x1 387 us: shards(): lax.all_gather(kv_slice[None], ('tensor', 'section'), axis=0, tiled=True)]
    unnamed x1 -> x0, blocking collectives: 182 us -> none
    pallas_call x0 -> x2, Pallas kernels: none -> 118 us  [the longest x1 70.3 us: shards(): pl.pallas_call(attend_kernel, out_shape=jax.ShapeDtypeStruct(resid.shape,...]
    dot_general x7 -> x0, matrix products: 60.5 us -> none  [the longest x1 20.2 us: shards(): jnp.einsum('tkgqc,kqrc->kgtr', query_five, key_table, preferred_element_t...]
    unnamed x37 -> x26, local copies, waits for them, and re-layouts: 44.3 us -> 6.94 us
    concatenate x4 -> x0, local copies, waits for them, and re-layouts: 32.6 us -> none  [swap_halves(): return jnp.concatenate([-inputs[:, middle:], inputs[:, :middle]], axis=1)]
    unnamed x8 -> x0, starting transfers between devices: 26.1 us -> none
    convert_element_type x3 -> x0, local copies, waits for them, and re-layouts: 17 us -> none  [the longest x1 16.2 us: shards(): raw_keys = split_cols[:, 0].astype(jnp.float32)]
  transfers between devices with their start and end apart: 11 -> 0, of which waited for: 5 -> 0; matrix products, arithmetic and copies ran while one was open for 2% -> 0% of each run, Pallas kernels for 0% -> 0%
where the time goes in v1:
time: 131 us; the launch traced here: 130 us
  Pallas kernels  118 us (90%)
  local copies, waits for them, and re-layouts  6.95 us (5%)
  other arithmetic  5.1 us (4%)
    pallas_call x1, Pallas kernels, shards(): pl.pallas_call(attend_kernel, out_shape=jax.ShapeDtypeStruct(resid.shape,...  70.3 us
    pallas_call x1, Pallas kernels, shards(): pl.pallas_call(project_kernel, out_shape=(jax.ShapeDtypeStruct((QC, TOK),...  47.7 us
    unnamed x26, local copies, waits for them, and re-layouts  6.94 us

profile of v1, /device:TPU:192, one launch (start us, length us, event | category | flops | bytes accessed | tf_op | source)
XLA Modules:
  0.0 130.2 jit_solution(17001167008954209674)
XLA Ops:
  0.0 0.8 reduce-window.9
  0.8 0.7 fusion
  1.5 0.8 multiply_cosine_fusion.1
  2.3 1.0 multiply_add_fusion
  3.3 0.0 copy-start.10
  3.3 0.0 copy-start.2
  3.3 0.0 copy-start.4
  3.3 0.0 copy-start.6
  3.4 0.0 copy-start.7
  3.4 0.0 copy-start.8
  3.4 2.2 %copy.15.kv_hbm = bf16[8192,64]{1,0:T(8,128)(2,1)S(1)} copy(bf16[8192,64]{0,1:T(8,128)(2,1)} %param.17) | data formatting | bytes 2097152 | tf_op args[4]
  5.5 0.0 copy-start.11
  5.6 0.0 copy-start.3
  5.6 0.0 copy-start.9
  5.6 0.8 fusion.1
  6.4 0.0 copy-start
  6.4 2.2 %copy-done = bf16[8192,256]{1,0:T(8,128)(2,1)S(1)} copy-done((bf16[8192,256]{1,0:T(8,128)(2,1)S(1)}, bf16[8192,256]{1,0:T(8,128)(2,1)}, u32[]{:S(2)}) %copy-start) | copy-done | bytes 4194328
  8.6 0.0 copy-start.1
  8.6 0.9 copy-done.1
  9.5 0.0 copy-start.5
  9.5 0.9 copy-done.5
  10.4 47.7 %project.1 = (bf16[256,384]{1,0:T(8,128)(2,1)S(1)}, bf16[64,384]{1,0:T(8,128)(2,1)S(1)}) custom-call(bf16[1,12,8192]{2,1,0:T(8,128)(2,1)S(1)} %copy-done.1, f32[1,8192]{1,0:T(1,128)S(1)} %bitcast.11, bf16[384,128]{1,0:T(8,128)(2,1)S(1)} %copy-done.5, bf16[8192,256]{1,0:T(8,128)(2,1)S(1)} %copy-done, bf16[8192,64]{1,0:T(8,128)(2,1)S(1)} %copy.15.kv_hbm, ...), custom_call_target="tpu_custom_call" | custom-call | tf_op jit(solution)/shard_map/project/pallas_call | solution.py:506
  58.2 0.0 copy-done.11
  58.2 1.0 multiply_sine_fusion
  59.2 0.0 copy-done.10
  59.2 0.0 copy-done.2
  59.2 0.0 copy-done.4
  59.2 0.0 copy-done.6
  59.2 0.0 copy-done.7
  59.2 0.0 copy-done.8
  59.3 0.0 copy-done.3
  59.3 0.0 copy-done.9
  59.3 70.3 %attend.1 = bf16[1,12,8192]{2,1,0:T(8,128)(2,1)S(1)} custom-call(s32[8]{0:T(128)S(1)} %copy-done.9, bf16[256,384]{1,0:T(8,128)(2,1)S(1)} %get-tuple-element.7.q_ref, bf16[64,384]{1,0:T(8,128)(2,1)S(1)} %get-tuple-element.8.kv_ref, f32[8,64,1]{2,1,0:T(8,128)S(1)} %get-tuple-element.12.off_cos, f32[8,64,1]{2,1,0:T(8,128)S(1)} %get-tuple-element.11.off_sin, ...), custom_call_target="tpu_custom_call" | custom-call | tf_op jit(solution)/shard_map/attend/pallas_call | solution.py:537
  129.5 0.7 copy.18
  (2 shorter events, 0.0 us)
Async XLA Ops:
  3.3 55.9 %copy-start.10 = (s32[8192]{0:T(1024)S(1)}, s32[8192]{0:T(1024)}, u32[]{:S(2)}) copy-start(s32[8192]{0:T(1024)} %param.15) | copy-start | bytes 98308
  3.3 55.9 %copy-start.2 = (bf16[1,12,8192]{2,1,0:T(8,128)(2,1)S(1)}, bf16[1,12,8192]{2,1,0:T(8,128)(2,1)}, u32[]{:S(2)}) copy-start(bf16[1,12,8192]{2,1,0:T(8,128)(2,1)} %resid.3) | copy-start | bytes 589828
  3.3 55.9 %copy-start.4 = (f32[64,384]{1,0:T(8,128)S(1)}, f32[64,384]{1,0:T(8,128)}, u32[]{:S(2)}) copy-start(f32[64,384]{1,0:T(8,128)} %constant.33.clone.tok_sin) | copy-start | bytes 294916
  3.3 55.9 %copy-start.6 = (bf16[384,128]{1,0:T(8,128)(2,1)S(1)}, bf16[384,128]{1,0:T(8,128)(2,1)}, u32[]{:S(2)}) copy-start(bf16[384,128]{1,0:T(8,128)(2,1)} %constant.35.clone.had) | copy-start | bytes 294916
  3.4 55.9 %copy-start.7 = (s32[384,1]{1,0:T(8,128)S(1)}, s32[384,1]{1,0:T(8,128)}, u32[]{:S(2)}) copy-start(s32[384,1]{1,0:T(8,128)} %constant.36.clone.key_tok) | copy-start | bytes 4612
  3.4 55.9 %copy-start.8 = (s32[1,768]{1,0:T(1,128)S(1)}, s32[1,768]{1,0:T(1,128)}, u32[]{:S(2)}) copy-start(s32[1,768]{1,0:T(1,128)} %constant.37.clone.query_tok) | copy-start | bytes 9220
  5.5 52.6 %copy-start.11 = (f32[64]{0:T(128)S(1)}, f32[64]{0:T(128)}, u32[]{:S(2)}) copy-start(f32[64]{0:T(128)} %constant.34.clone) | copy-start | bytes 772
  5.6 53.7 %copy-start.3 = (f32[64,384]{1,0:T(8,128)S(1)}, f32[64,384]{1,0:T(8,128)}, u32[]{:S(2)}) copy-start(f32[64,384]{1,0:T(8,128)} %constant.32.clone.tok_cos) | copy-start | bytes 294916
  5.6 53.7 %copy-start.9 = (s32[8]{0:T(128)S(1)}, s32[8]{0:T(128)}, u32[]{:S(2)}) copy-start(s32[8]{0:T(128)} %lengths.1) | copy-start | bytes 100
  6.4 2.2 %copy-start = (bf16[8192,256]{1,0:T(8,128)(2,1)S(1)}, bf16[8192,256]{1,0:T(8,128)(2,1)}, u32[]{:S(2)}) copy-start(bf16[8192,256]{1,0:T(8,128)(2,1)} %q_hbm.1) | copy-start | bytes 12582916
  8.6 0.9 copy-start.1
  9.5 0.9 copy-start.5

commit v2 on v1

v2 whole, which is shorter than its diff:
```python
import functools
import math

import jax
import jax.numpy as jnp
import numpy as np
from jax import lax
from jax.experimental import pallas as pl
from jax.experimental.pallas import tpu as pltpu
from jax.sharding import PartitionSpec as P

MESH = pl.DeviceIdType.MESH
D = 8192
HD = 128
HB = 128
ROWS = 12
TOK = 384
BLOCKS = 8
NC = 4
HALF = D // 2
CW = HALF // NC
SUB = 4
SW = CW // SUB
PR = SUB * ROWS
QC = 256
KC = 64
rope_base = 500000.0
norm_eps = 1e-05
NEG = -1e30


def hadamard(extent):
    index = np.arange(extent)
    bits = index[:, None] & index[None, :]
    parity = np.zeros((extent, extent), np.int64)
    while bits.any():
        parity += bits & 1
        bits = bits >> 1
    return (1 - 2 * (parity % 2)).astype(np.float32)


def token_order():
    order = []
    for half in range(2):
        for j in range(4):
            for i in range(4):
                y, x = (j, i) if half == 0 else (i, j)
                t = (y * 4 + x) * 2 + half
                order.extend(range(t * ROWS, (t + 1) * ROWS))
    return np.array(order)


def here():
    t = lax.axis_index("tensor")
    s = lax.axis_index("section")
    y = t // 8
    x = lax.rem(t // 2, 4)
    z = (s // 2) * 2 + lax.rem(t, 2)
    return y, x, z, lax.rem(s, 2)


def device(y, x, z, c):
    return ((y * 4 + x) * 2 + lax.rem(z, 2), (z // 2) * 2 + c)


def shift(value, by, size):
    return lax.rem(value + (by + size), size)


def split3(value):
    high = value.astype(jnp.bfloat16)
    rest = value - high.astype(jnp.float32)
    middle = rest.astype(jnp.bfloat16)
    low = (rest - middle.astype(jnp.float32)).astype(jnp.bfloat16)
    return jnp.concatenate([high, middle, low], axis=1)


def greet(partners):
    barrier = pltpu.get_barrier_semaphore()
    for partner in partners:
        pl.semaphore_signal(barrier, inc=1, device_id=partner, device_id_type=MESH)
    pl.semaphore_wait(barrier, len(partners))


def remote(src, dst, send, recv, target):
    return pltpu.make_async_remote_copy(
        src_ref=src,
        dst_ref=dst,
        send_sem=send,
        recv_sem=recv,
        device_id=target,
        device_id_type=MESH,
    )


def sublayer_kernel(
    lengths, resid, gain, signs, had, inverse, tok_cos, tok_sin, key_tok, query_tok,
    q_hbm, kv_hbm, out_hbm, mixed,
    wq, wkv, wo, rot, p2, blocks, acc_q, acc_kv, cross, crossed, queries, off_cos, off_sin,
    kvs, top_ref, total_ref, acc, att, parts, raw1, fin1, parts2, raw2, fin2, sums, sums_bf, last_z, full,
    w_sem, swq, rwq, swo, rwo, sa, ra, sg2, rg2, sg3, rg3, scr, rcr, sx, rx, skv, rkv, sc, rc,
    sat, rat, s1, r1, s2, r2, sz, rz,
):
    y, x, z, core = here()
    low = lax.rem(z, 2)
    high = z // 2
    section = lax.axis_index("section")
    toward = 1 - 2 * low

    def at_x(by):
        return device(y, shift(x, by, 4), z, core)

    def at_y(by):
        return device(shift(y, by, 4), x, z, core)

    def at_z(by):
        return device(y, x, shift(z, by, 8), core)

    mate = at_z(toward)
    other_core = device(y, x, z, 1 - core)
    own_x = lax.rem(x, 2)
    x_mate = device(y, x + 1 - 2 * own_x, z, core)

    def ring_x(h, by):
        return device(shift(y, by * h, 4), shift(x, by * (1 - h), 4), z, core)

    def ring_y(h, by):
        return device(shift(y, by * (1 - h), 4), shift(x, by * h, 4), z, core)

    def pos_x(h):
        return x * (1 - h) + y * h

    def pos_y(h):
        return y * (1 - h) + x * h

    started = []

    def go(copy):
        copy.start()
        started.append(copy)

    greet([at_z(1), at_z(-1), other_core, at_x(1), at_x(-1), at_y(1), at_y(-1)])

    mine = pl.multiple_of(low * HALF, HALF)
    loads = [
        pltpu.make_async_copy(q_hbm.at[pl.ds(mine, HALF)], wq.at[0], w_sem.at[0]),
        pltpu.make_async_copy(kv_hbm.at[:, pl.ds(mine, HALF)], wkv.at[0], w_sem.at[1]),
        pltpu.make_async_copy(out_hbm.at[:, pl.ds(mine, HALF)], wo.at[0], w_sem.at[2]),
    ]
    QTR = HALF // 4

    def quarter(way, c):
        return (way * 2 + c) * QTR

    def ship_proj(way):
        target = at_z(toward * (1 - 2 * way))
        off = quarter(way, core)
        from_ = pl.multiple_of((1 - low) * HALF + off, QTR)
        to = pl.multiple_of(off, QTR)
        go(remote(q_hbm.at[pl.ds(from_, QTR)], wq.at[1, pl.ds(to, QTR)], swq.at[way, 0], rwq.at[way, 0], target))
        go(remote(kv_hbm.at[:, pl.ds(from_, QTR)], wkv.at[1, :, pl.ds(to, QTR)], swq.at[way, 1], rwq.at[way, 1], target))

    def share_proj(way):
        to = pl.multiple_of(quarter(way, core), QTR)
        q_ref, kv_ref = wq.at[1, pl.ds(to, QTR)], wkv.at[1, :, pl.ds(to, QTR)]
        remote(q_ref, q_ref, swq.at[way, 0], rwq.at[way, 0], mate).wait_recv()
        remote(kv_ref, kv_ref, swq.at[way, 1], rwq.at[way, 1], mate).wait_recv()
        go(remote(q_ref, q_ref, swq.at[2 + way, 0], rwq.at[2 + way, 0], other_core))
        go(remote(kv_ref, kv_ref, swq.at[2 + way, 1], rwq.at[2 + way, 1], other_core))

    def shared_proj(way):
        to = pl.multiple_of(quarter(way, 1 - core), QTR)
        q_ref, kv_ref = wq.at[1, pl.ds(to, QTR)], wkv.at[1, :, pl.ds(to, QTR)]
        remote(q_ref, q_ref, swq.at[2 + way, 0], rwq.at[2 + way, 0], other_core).wait_recv()
        remote(kv_ref, kv_ref, swq.at[2 + way, 1], rwq.at[2 + way, 1], other_core).wait_recv()

    def ship_out(way):
        target = at_z(toward * (1 - 2 * way))
        off = quarter(way, core)
        from_ = pl.multiple_of((1 - low) * HALF + off, QTR)
        to = pl.multiple_of(off, QTR)
        go(remote(out_hbm.at[:, pl.ds(from_, QTR)], wo.at[1, :, pl.ds(to, QTR)], swo.at[way], rwo.at[way], target))

    def share_out(way):
        ref = wo.at[1, :, pl.ds(pl.multiple_of(quarter(way, core), QTR), QTR)]
        remote(ref, ref, swo.at[way], rwo.at[way], mate).wait_recv()
        go(remote(ref, ref, swo.at[2 + way], rwo.at[2 + way], other_core))

    def shared_out(way):
        ref = wo.at[1, :, pl.ds(pl.multiple_of(quarter(way, 1 - core), QTR), QTR)]
        remote(ref, ref, swo.at[2 + way], rwo.at[2 + way], other_core).wait_recv()

    ship_proj(1)
    for load in loads:
        load.start()

    stream = resid[0].astype(jnp.float32)
    sign_row = (2 * signs[...] - 1).astype(jnp.float32)
    normed = (
        stream
        * lax.rsqrt(jnp.mean(stream * stream, axis=-1, keepdims=True) + norm_eps)
        * gain[...]
        * sign_row
    )
    per = SW // HB
    stacked = []
    for g in range(2 * NC):
        for b in range(per):
            stacked.append(
                jnp.concatenate(
                    [
                        normed[:, g * CW + j * SW + b * HB : g * CW + j * SW + (b + 1) * HB]
                        for j in range(SUB)
                    ],
                    axis=0,
                )
            )
    rotated = jnp.dot(
        split3(jnp.concatenate(stacked, axis=0)), had[...], preferred_element_type=jnp.float32
    ) * (1.0 / math.sqrt(HB))
    for g in range(2 * NC):
        blocks_of = [rotated[(g * per + b) * PR : (g * per + b + 1) * PR] for b in range(per)]
        rot[g // NC, g % NC] = jnp.concatenate(blocks_of, axis=1).astype(jnp.bfloat16)

    def swap_copy(c, h):
        return remote(
            rot.at[1 - low, c], p2.at[h, pos_x(h), c], sa.at[c], ra.at[c], mate
        )

    def direct(buf, pos, ssem, rsem, peer, h, c):
        ref = buf.at[h, pos(h), c]
        go(remote(ref, ref, ssem.at[h, 0, c], rsem.at[h, 0, c], peer(h, 1)))
        go(remote(ref, ref, ssem.at[h, 1, c], rsem.at[h, 1, c], peer(h, -1)))

    def arrive(buf, pos, ssem, rsem, peer, h, c):
        for kind, by in ((0, -1), (1, 1)):
            ref = buf.at[h, shift(pos(h), by, 4), c]
            remote(ref, ref, ssem.at[h, kind, c], rsem.at[h, kind, c], peer(h, 1)).wait_recv()
        by = -1 if c % 2 == 0 else 1
        ref = buf.at[h, shift(pos(h), by, 4), c]
        go(remote(ref, ref, ssem.at[h, 2, c], rsem.at[h, 2, c], peer(h, -by)))

    def last(buf, pos, ssem, rsem, peer, h, c):
        ref = buf.at[h, shift(pos(h), 2, 4), c]
        remote(ref, ref, ssem.at[h, 2, c], rsem.at[h, 2, c], peer(h, 1)).wait_recv()

    gather2 = (p2, pos_x, sg2, rg2, ring_x)
    gather3 = (blocks, pos_y, sg3, rg3, ring_y)
    for c in range(NC):
        go(swap_copy(c, low))
        p2[low, pos_x(low), c] = rot[low, c]
        direct(*gather2, low, c)
    ship_proj(0)
    for way in (1, 0):
        ship_out(way)
    for c in range(NC):
        swap_copy(c, 1 - low).wait_recv()
        direct(*gather2, 1 - low, c)
    for c in range(NC + 1):
        if c < NC:
            for h in range(2):
                arrive(*gather2, h, c)
        if c > 0:
            for h in range(2):
                last(*gather2, h, c - 1)
                pieces = [p2[h, i, c - 1].astype(jnp.float32) for i in range(4)]
                joined = jnp.concatenate(
                    [
                        jnp.concatenate(
                            [piece[j * ROWS : (j + 1) * ROWS] for piece in pieces], axis=0
                        )
                        for j in range(SUB)
                    ],
                    axis=1,
                )
                blocks[h, pos_y(h), c - 1] = joined.astype(jnp.bfloat16)
                direct(*gather3, h, c - 1)
    for load in loads:
        load.wait()

    def add_q(kind, c):
        part = jnp.dot(
            blocks[:, :, c].reshape(TOK, CW),
            wq[kind, c * CW : (c + 1) * CW],
            preferred_element_type=jnp.float32,
        )
        acc_q[kind] = part if c == 0 else acc_q[kind] + part

    def add_kv(c):
        part = lax.dot_general(
            blocks[:, :, c].reshape(TOK, CW),
            wkv[:, :, c * CW : (c + 1) * CW].reshape(2 * KC, CW),
            (((1,), (1,)), ((), ())),
            preferred_element_type=jnp.float32,
        )
        acc_kv[...] = part if c == 0 else acc_kv[...] + part

    lane = lax.broadcasted_iota(jnp.int32, (1, HB), 1)
    starts = jnp.zeros((1, HB), jnp.int32)
    for b in range(BLOCKS - 1):
        starts = starts + jnp.where(lane > b, lengths[b], 0)
    angles = inverse[...] * starts.astype(jnp.float32)
    off_cos[...] = jnp.cos(angles)
    off_sin[...] = jnp.sin(angles)

    def rotary_table(index):
        here_only = lane == index
        oc = jnp.sum(jnp.where(here_only, off_cos[...], 0.0), axis=1, keepdims=True)
        os = jnp.sum(jnp.where(here_only, off_sin[...], 0.0), axis=1, keepdims=True)
        return oc * tok_cos[...] - os * tok_sin[...], os * tok_cos[...] + oc * tok_sin[...]

    for c in range(NC):
        for h in range(2):
            arrive(*gather3, h, c)
        if c > 0:
            for h in range(2):
                last(*gather3, h, c - 1)
            if c < NC - 1:
                add_q(0, c - 1)
        if c == 1:
            share_proj(1)
        if c == 2:
            share_proj(0)
    for way in range(2):
        shared_proj(way)
    for c in range(NC - 1):
        add_kv(c)
        add_q(1, c)
    add_q(0, NC - 2)
    for h in range(2):
        last(*gather3, h, NC - 1)
    half = HD // 2

    def cross_copy(k):
        rows = pl.ds(0, KC) if k == 0 else pl.ds(KC, QC)
        return remote(cross.at[rows], crossed.at[rows], scr.at[k], rcr.at[k], mate)

    add_kv(NC - 1)
    kv_sum = jnp.transpose(acc_kv[...])
    cross[:KC] = kv_sum[KC:].astype(jnp.bfloat16)
    go(cross_copy(0))
    add_q(1, NC - 1)
    cross[KC:] = jnp.transpose(acc_q[1]).astype(jnp.bfloat16)
    go(cross_copy(1))

    def side(e):
        return own_x if e == 0 else 1 - own_x

    def hop(e, src_by, kind, dist, target):
        ref = kvs.at[core, side(e), shift(z, src_by, 8)]
        return remote(ref, ref, skv.at[kind, dist, e], rkv.at[kind, dist, e], target)

    def core_copy(e, k):
        ref = kvs.at[core, side(e), lax.rem(z + k, 8)]
        return remote(ref, ref, sc.at[e, k], rc.at[e, k], other_core)

    cross_copy(0).wait_recv()
    kvs[core, own_x, z] = (kv_sum[:KC] + crossed[:KC].astype(jnp.float32)).astype(jnp.bfloat16)
    own = kvs.at[core, own_x, z]
    go(remote(own, own, sx, rx, x_mate))
    go(hop(0, 0, 0, 0, at_z(1)))
    go(hop(0, 0, 1, 0, at_z(-1)))
    go(core_copy(0, 0))
    add_q(0, NC - 1)
    theirs = kvs.at[core, 1 - own_x, z]
    remote(theirs, theirs, sx, rx, x_mate).wait_recv()
    go(hop(1, 0, 0, 0, at_z(1)))
    go(hop(1, 0, 1, 0, at_z(-1)))
    go(core_copy(1, 0))

    cross_copy(1).wait_recv()
    turned = jnp.transpose(acc_q[0]) + crossed[KC:].astype(jnp.float32)
    cosine, sine = rotary_table(section)
    for head in range(2):
        first = turned[head * HD : head * HD + half]
        second = turned[head * HD + half : (head + 1) * HD]
        queries[:half, head * TOK : (head + 1) * TOK] = (
            first * cosine - second * sine
        ).astype(jnp.bfloat16)
        queries[half:, head * TOK : (head + 1) * TOK] = (
            second * cosine + first * sine
        ).astype(jnp.bfloat16)

    def ring_step(dist):
        for e in range(2):
            for kind, sgn in ((0, -1), (1, 1)):
                if dist == 3 and kind != e:
                    continue
                by = sgn * (dist + 1)
                hop(e, by, kind, dist, mate).wait_recv()
                if dist < 2 or (dist == 2 and kind == e):
                    go(hop(e, by, kind, dist + 1, at_z(-sgn)))
                go(core_copy(e, by % 8))

    def from_core(back):
        for u in range(2):
            k = shift(u - low, -2 * back + 8, 8)
            for e in range(2):
                ref = kvs.at[1 - core, side(e), lax.rem(z + k, 8)]
                remote(ref, ref, sc.at[e, k], rc.at[e, k], other_core).wait_recv()

    scale = math.log2(math.e) / math.sqrt(HD)

    def absorb(c, row, diagonal):
        index = row * 2 + c
        pair = pl.ds(row * 2, 2)
        raw = kvs[c, 0, pair].astype(jnp.float32)
        value = kvs[c, 1, pair].reshape(HD, TOK)
        cosine, sine = rotary_table(index)
        key = jnp.concatenate(
            [raw[0] * cosine - raw[1] * sine, raw[1] * cosine + raw[0] * sine], axis=0
        )
        key = jnp.transpose(key).astype(jnp.bfloat16)
        scores = jnp.dot(key, queries[...], preferred_element_type=jnp.float32)
        valid = key_tok[...] < lengths[index]
        if diagonal:
            seen = valid & (key_tok[...] <= query_tok[...])
            scores = jnp.where(seen, scores, NEG)
            top = jnp.max(scores, axis=0, keepdims=True)
            weights = jnp.exp2((scores - top) * scale)
            total_ref[...] = jnp.sum(weights, axis=0, keepdims=True)
            acc[...] = jnp.dot(
                value, weights.astype(jnp.bfloat16), preferred_element_type=jnp.float32
            )
        else:
            scores = scores + jnp.where(valid, 0.0, NEG)
            old = top_ref[...]
            top = jnp.maximum(old, jnp.max(scores, axis=0, keepdims=True))
            weights = jnp.exp2((scores - top) * scale)
            fade = jnp.exp2((old - top) * scale)
            total_ref[...] = total_ref[...] * fade + jnp.sum(weights, axis=0, keepdims=True)
            acc[...] = acc[...] * fade + jnp.dot(
                value, weights.astype(jnp.bfloat16), preferred_element_type=jnp.float32
            )
        top_ref[...] = top

    def earlier(back):
        @pl.when(high >= back)
        def _():
            for c in range(2):
                absorb(c, high - back, False)

    ring_step(0)
    from_core(0)
    absorb(core, high, True)

    @pl.when(core == 1)
    def _():
        absorb(0, high, False)

    ring_step(1)
    ring_step(2)
    from_core(1)
    from_core(3)
    earlier(1)
    earlier(3)
    ring_step(3)
    from_core(2)
    for way in range(2):
        share_out(way)
    earlier(2)
    attended = acc[...] / total_ref[...]
    for head in range(2):
        att[0, :, head * HD : (head + 1) * HD] = jnp.transpose(
            attended[:, head * TOK : (head + 1) * TOK]
        ).astype(jnp.bfloat16)
    att_copy = remote(att.at[0], att.at[1], sat, rat, mate)
    go(att_copy)
    for way in range(2):
        shared_out(way)
    att_copy.wait_recv()

    def send_raw(buf, raw, fin, pos, ssem, rsem, peer, h, c):
        by = 1 if c % 2 == 0 else -1
        go(
            remote(
                buf.at[h, shift(pos(h), 2, 4), c], raw.at[h, c], ssem.at[h, 2, c],
                rsem.at[h, 2, c], peer(h, by),
            )
        )

    def send_fin(buf, raw, fin, pos, ssem, rsem, peer, h, c, kind):
        by = 1 if kind == 0 else -1
        go(
            remote(
                buf.at[h, shift(pos(h), by, 4), c], fin.at[h, kind, c], ssem.at[h, kind, c],
                rsem.at[h, kind, c], peer(h, by),
            )
        )

    def pass_on(buf, raw, fin, pos, ssem, rsem, peer, h, c):
        kind, by = (0, 1) if c % 2 == 0 else (1, -1)
        ref = raw.at[h, c]
        remote(ref, ref, ssem.at[h, 2, c], rsem.at[h, 2, c], peer(h, 1)).wait_recv()
        slot = shift(pos(h), by, 4)
        buf[h, slot, c] = (
            buf[h, slot, c].astype(jnp.float32) + raw[h, c].astype(jnp.float32)
        ).astype(jnp.bfloat16)
        send_fin(buf, raw, fin, pos, ssem, rsem, peer, h, c, kind)

    def finish(buf, raw, fin, pos, ssem, rsem, peer, h, c):
        for kind in range(2):
            ref = fin.at[h, kind, c]
            remote(ref, ref, ssem.at[h, kind, c], rsem.at[h, kind, c], peer(h, 1)).wait_recv()
        return (
            buf[h, pos(h), c].astype(jnp.float32)
            + fin[h, 0, c].astype(jnp.float32)
            + fin[h, 1, c].astype(jnp.float32)
        )

    ring1 = (parts, raw1, fin1, pos_y, s1, r1, ring_y)
    ring2 = (parts2, raw2, fin2, pos_x, s2, r2, ring_x)
    for c in range(NC):
        columns = pl.ds(c * CW, CW)
        partial = jnp.dot(
            att[0], wo[0, :, columns], preferred_element_type=jnp.float32
        ) + jnp.dot(att[1], wo[1, :, columns], preferred_element_type=jnp.float32)
        parts[:, :, c] = partial.astype(jnp.bfloat16).reshape(2, 4, PR, CW)
        for h in range(2):
            send_raw(*ring1, h, c)
            send_fin(*ring1, h, c, 1 if c % 2 == 0 else 0)
    for c in range(NC):
        for h in range(2):
            pass_on(*ring1, h, c)

    def z_copy(c, h):
        return remote(sums_bf.at[h, c], last_z.at[c], sz.at[c], rz.at[c], mate)

    for c in range(NC + 2):
        if c < NC:
            for h in range(2):
                done = finish(*ring1, h, c)
                for i in range(4):
                    parts2[h, i, c] = jnp.concatenate(
                        [
                            done[i * ROWS : (i + 1) * ROWS, j * SW : (j + 1) * SW]
                            for j in range(SUB)
                        ],
                        axis=0,
                    ).astype(jnp.bfloat16)
                send_raw(*ring2, h, c)
                send_fin(*ring2, h, c, 1 if c % 2 == 0 else 0)
        if 0 < c <= NC:
            for h in range(2):
                pass_on(*ring2, h, c - 1)
        if c > 1:
            for h in range(2):
                done = finish(*ring2, h, c - 2)
                sums[h, c - 2] = done
                sums_bf[h, c - 2] = done.astype(jnp.bfloat16)
            go(z_copy(c - 2, 1 - low))
    full[low] = sums[low]
    for c in range(NC):
        z_copy(c, low).wait_recv()
        full[1 - low, c] = last_z[c].astype(jnp.float32)
    stacked = []
    for g in range(2 * NC):
        branch = full[g // NC, g % NC]
        stacked += [branch[:, b * HB : (b + 1) * HB] for b in range(per)]
    back = jnp.dot(
        split3(jnp.concatenate(stacked, axis=0)), had[...], preferred_element_type=jnp.float32
    ) * (1.0 / math.sqrt(HB))
    columns = []
    for g in range(2 * NC):
        for j in range(SUB):
            for b in range(per):
                row = (g * per + b) * PR + j * ROWS
                columns.append(back[row : row + ROWS])
    back = jnp.concatenate(columns, axis=1)
    sign_row = (2 * signs[...] - 1).astype(jnp.float32)
    mixed[0] = (resid[0].astype(jnp.float32) + sign_row * back).astype(jnp.bfloat16)
    for copy in started:
        copy.wait_send()


def vmem(shape, dtype):
    return pltpu.VMEM(shape, dtype)


def shards(resid, norm_gain, signs, query_weight, kv_weight, out_weight, lengths):
    bf16, f32 = jnp.bfloat16, jnp.float32
    dma = pltpu.SemaphoreType.DMA
    in_vmem = pl.BlockSpec(memory_space=pltpu.VMEM)
    in_any = pl.BlockSpec(memory_space=pl.ANY)
    order = token_order()
    inverse = np.exp(np.arange(HD // 2) * (-2.0 * math.log(rope_base) / HD))
    angles = inverse[:, None] * order[None, :]
    had = hadamard(HB)
    ring = dma((2, 3, NC))
    return pl.pallas_call(
        sublayer_kernel,
        out_shape=jax.ShapeDtypeStruct(resid.shape, bf16),
        in_specs=[pl.BlockSpec(memory_space=pltpu.SMEM)] + [in_vmem] * 9 + [in_any] * 3,
        out_specs=in_vmem,
        scratch_shapes=[
            vmem((2, HALF, QC), bf16),
            vmem((2, KC, HALF), bf16),
            vmem((2, QC, HALF), bf16),
            vmem((2, NC, PR, SW), bf16),
            vmem((2, 4, NC, PR, SW), bf16),
            vmem((2, 4, NC, PR, CW), bf16),
            vmem((2, TOK, QC), f32),
            vmem((TOK, 2 * KC), f32),
            vmem((KC + QC, TOK), bf16),
            vmem((KC + QC, TOK), bf16),
            vmem((HD, 2 * TOK), bf16),
            vmem((HD // 2, HB), f32),
            vmem((HD // 2, HB), f32),
            vmem((2, 2, 8, KC, TOK), bf16),
            vmem((1, 2 * TOK), f32),
            vmem((1, 2 * TOK), f32),
            vmem((HD, 2 * TOK), f32),
            vmem((2, TOK, QC), bf16),
            vmem((2, 4, NC, PR, CW), bf16),
            vmem((2, NC, PR, CW), bf16),
            vmem((2, 2, NC, PR, CW), bf16),
            vmem((2, 4, NC, PR, SW), bf16),
            vmem((2, NC, PR, SW), bf16),
            vmem((2, 2, NC, PR, SW), bf16),
            vmem((2, NC, PR, SW), f32),
            vmem((2, NC, PR, SW), bf16),
            vmem((NC, PR, SW), bf16),
            vmem((2, NC, PR, SW), f32),
            dma((3,)),
            dma((4, 2)),
            dma((4, 2)),
            dma((4,)),
            dma((4,)),
            dma((NC,)),
            dma((NC,)),
            ring,
            ring,
            ring,
            ring,
            dma((2,)),
            dma((2,)),
            dma,
            dma,
            dma((2, 4, 2)),
            dma((2, 4, 2)),
            dma((2, 8)),
            dma((2, 8)),
            dma,
            dma,
            ring,
            ring,
            ring,
            ring,
            dma((NC,)),
            dma((NC,)),
        ],
        compiler_params=pltpu.CompilerParams(
            collective_id=1, has_side_effects=True, vmem_limit_bytes=50 << 20
        ),
        name="sublayer",
    )(
        lengths, resid, norm_gain[None, :], signs[None, :],
        jnp.asarray(np.concatenate([had, had, had], axis=0), bf16),
        jnp.asarray(inverse[:, None], f32),
        jnp.asarray(np.cos(angles), f32), jnp.asarray(np.sin(angles), f32),
        jnp.asarray(order[:, None], jnp.int32),
        jnp.asarray(np.concatenate([order, order])[None, :], jnp.int32),
        query_weight, kv_weight.T, out_weight,
    )


def solution(mesh):
    return jax.shard_map(
        shards,
        mesh=mesh,
        in_specs=(
            P("section", "tensor", None),
            P(),
            P(),
            P(None, "tensor"),
            P(None, "tensor"),
            P("tensor", None),
            P(),
        ),
        out_specs=P("section", "tensor", None),
        check_vma=False,
    )
```

time: 131 us -> 109 us (0.83)
  Pallas kernels: 118 us -> 98.8 us
  other arithmetic: 5.1 us -> 0 us
  local copies, waits for them, and re-layouts: 6.95 us -> 10.1 us
    pallas_call x2 -> x1, Pallas kernels: 118 us -> 98.8 us  [shards(): pl.pallas_call(sublayer_kernel, out_shape=jax.ShapeDtypeStruct(resid.shap...]
    unnamed x26 -> x23, local copies, waits for them, and re-layouts: 6.94 us -> 10.1 us
where the time goes in v2:
time: 109 us
  Pallas kernels  98.8 us (91%)
  local copies, waits for them, and re-layouts  10.1 us (9%)
    pallas_call x1, Pallas kernels, shards(): pl.pallas_call(sublayer_kernel, out_shape=jax.ShapeDtypeStruct(resid.shap...  98.8 us
    unnamed x23, local copies, waits for them, and re-layouts  10.1 us

profile of v2, /device:TPU:192, one launch (start us, length us, event | category | flops | bytes accessed | tf_op | source)
XLA Modules:
  0.0 108.9 jit_solution(7720705072987709094)
XLA Ops:
  0.0 0.0 copy-start
  0.0 1.2 %copy-done = bf16[8192,64]{0,1:T(8,128)(2,1)S(1)} copy-done((bf16[8192,64]{0,1:T(8,128)(2,1)S(1)}, bf16[8192,64]{0,1:T(8,128)(2,1)}, u32[]{:S(2)}) %copy-start) | copy-done | bytes 1048600
  1.2 0.0 copy-start.1
  1.2 0.9 copy-done.1
  2.2 0.0 copy-start.2
  2.2 0.9 copy-done.2
  3.1 0.0 copy-start.3
  3.1 0.9 copy-done.3
  4.0 0.0 copy-start.4
  4.0 0.9 copy-done.4
  4.9 0.0 copy-start.5
  4.9 0.9 copy-done.5
  5.8 0.0 copy-start.6
  5.8 0.8 copy-done.6
  6.5 0.0 copy-start.7
  6.5 0.8 copy-done.7
  7.3 0.0 copy-start.8
  7.3 0.8 copy-done.8
  8.1 0.0 copy-start.9
  8.1 0.7 copy-done.9
  8.7 0.0 copy-start.10
  8.7 0.7 copy-done.10
  9.4 98.8 %sublayer.1 = bf16[1,12,8192]{2,1,0:T(8,128)(2,1)S(1)} custom-call(s32[8]{0:T(128)S(1)} %copy-done.10, bf16[1,12,8192]{2,1,0:T(8,128)(2,1)S(1)} %copy-done.1, f32[1,8192]{1,0:T(1,128)S(1)} %bitcast.4, s32[1,8192]{1,0:T(1,128)S(1)} %bitcast.5, bf16[384,128]{1,0:T(8,128)(2,1)S(1)} %copy-done.5, f32[64,1]{1,0:T(8,128)S(1)} %copy-done.8, ...), custom_call_target="tpu_custom_call" | custom-call | tf_op jit(solution)/shard_map/sublayer/pallas_call | solution.py:590
  108.2 0.7 copy.15
Async XLA Ops:
  0.0 1.2 %copy-start = (bf16[8192,64]{0,1:T(8,128)(2,1)S(1)}, bf16[8192,64]{0,1:T(8,128)(2,1)}, u32[]{:S(2)}) copy-start(bf16[8192,64]{0,1:T(8,128)(2,1)} %param.17) | copy-start | bytes 3145732
  1.2 0.9 copy-start.1
  2.2 0.9 copy-start.2
  3.1 0.9 copy-start.3
  4.0 0.9 copy-start.4
  4.9 0.9 copy-start.5
  5.8 0.8 copy-start.6
  6.5 0.8 copy-start.7
  7.3 0.8 copy-start.8
  8.1 0.7 copy-start.9
  8.7 0.7 copy-start.10

commit v3 on v2

v3 whole, which is shorter than its diff:
```python
import functools
import math

import jax
import jax.numpy as jnp
import numpy as np
from jax import lax
from jax.experimental import pallas as pl
from jax.experimental.pallas import tpu as pltpu
from jax.sharding import PartitionSpec as P

MESH = pl.DeviceIdType.MESH
D = 8192
HD = 128
HB = 128
ROWS = 12
TOK = 384
BLOCKS = 8
NC = 4
HALF = D // 2
CW = HALF // NC
SUB = 4
SW = CW // SUB
PR = SUB * ROWS
QC = 256
KC = 64
rope_base = 500000.0
norm_eps = 1e-05
NEG = -1e30


def token_order():
    order = []
    for half in range(2):
        for i in range(4):
            for j in range(4):
                y, x = (j, i) if half == 0 else (i, j)
                t = (y * 4 + x) * 2 + half
                order.extend(range(t * ROWS, (t + 1) * ROWS))
    return np.array(order)


def here():
    t = lax.axis_index("tensor")
    s = lax.axis_index("section")
    y = t // 8
    x = lax.rem(t // 2, 4)
    z = (s // 2) * 2 + lax.rem(t, 2)
    return y, x, z, lax.rem(s, 2)


def device(y, x, z, c):
    return ((y * 4 + x) * 2 + lax.rem(z, 2), (z // 2) * 2 + c)


def shift(value, by, size):
    return lax.rem(value + (by + size), size)


def split3(value):
    high = value.astype(jnp.bfloat16)
    rest = value - high.astype(jnp.float32)
    middle = rest.astype(jnp.bfloat16)
    low = (rest - middle.astype(jnp.float32)).astype(jnp.bfloat16)
    return jnp.concatenate([high, middle, low], axis=1)


def greet(partners):
    barrier = pltpu.get_barrier_semaphore()
    for partner in partners:
        pl.semaphore_signal(barrier, inc=1, device_id=partner, device_id_type=MESH)


def met(partners):
    pl.semaphore_wait(pltpu.get_barrier_semaphore(), len(partners))


def remote(src, dst, send, recv, target):
    return pltpu.make_async_remote_copy(
        src_ref=src,
        dst_ref=dst,
        send_sem=send,
        recv_sem=recv,
        device_id=target,
        device_id_type=MESH,
    )


def sublayer_kernel(
    lengths_hbm, resid_hbm, gain_hbm, signs_hbm, table_hbm, q_hbm, kv_hbm, out_hbm, mixed,
    lengths, resid, gain, signs, table, had, key_tok, wq, wkv, wo, rot, pieces, rows_ref, acc_q, acc_kv, cross_q, cross_kv, crossed_q, crossed_kv, queries, off_cos, off_sin,
    kvs, top_ref, total_ref, acc, att, parts, raw1, fin1, parts2, fin2, full,
    in_sem, w_sem, swq, rwq, swo, rwo, sa, ra, sg2, rg2, sg3, rg3, scr, rcr, sx, rx, skv, rkv, sc, rc,
    sat, rat, s1, r1, s2, r2,
):
    y, x, z, core = here()
    low = lax.rem(z, 2)
    high = z // 2
    section = lax.axis_index("section")
    toward = 1 - 2 * low

    def at_x(by):
        return device(y, shift(x, by, 4), z, core)

    def at_y(by):
        return device(shift(y, by, 4), x, z, core)

    def at_z(by):
        return device(y, x, shift(z, by, 8), core)

    mate = at_z(toward)
    other_core = device(y, x, z, 1 - core)
    own_x = lax.rem(x, 2)

    def x_mate_at(by):
        return device(y, x + 1 - 2 * own_x, shift(z, by, 8), core)

    x_mate = x_mate_at(0)

    def ring_x(h, by):
        return device(shift(y, by * h, 4), shift(x, by * (1 - h), 4), z, core)

    def ring_y(h, by):
        return device(shift(y, by * (1 - h), 4), shift(x, by * h, 4), z, core)

    def pos_x(h):
        return x * (1 - h) + y * h

    def pos_y(h):
        return y * (1 - h) + x * h

    started = []

    def go(copy):
        copy.start()
        started.append(copy)

    def beyond(by):
        h = 1 - low
        return device(shift(y, by * h, 4), shift(x, by * (1 - h), 4), shift(z, toward, 8), core)

    def behind(by):
        return device(
            shift(y, by * low, 4), shift(x, by * (1 - low), 4), shift(z, toward, 8), core
        )

    partners = [at_z(by) for by in (1, -1, 2, -2)] + [other_core]
    partners += [at_x(by) for by in (1, -1, 2)] + [at_y(by) for by in (1, -1, 2)]
    partners += [behind(by) for by in (1, -1, 2)]
    partners += [x_mate_at(by) for by in (1, -1, 2, -2)]
    greet(partners)
    inputs = [
        pltpu.make_async_copy(from_, to, in_sem.at[k])
        for k, (from_, to) in enumerate(
            [
                (resid_hbm, resid), (gain_hbm, gain), (signs_hbm, signs), (lengths_hbm, lengths),
                (table_hbm, table),
            ]
        )
    ]
    for copy in inputs:
        copy.start()

    mine = pl.multiple_of(low * HALF, HALF)
    loads = [
        pltpu.make_async_copy(q_hbm.at[pl.ds(mine, HALF)], wq.at[0], w_sem.at[0]),
        pltpu.make_async_copy(kv_hbm.at[:, pl.ds(mine, HALF)], wkv.at[0], w_sem.at[1]),
        pltpu.make_async_copy(out_hbm.at[:, pl.ds(mine, HALF)], wo.at[0], w_sem.at[2]),
    ]
    QTR = HALF // 4

    def quarter(way, c):
        return (way * 2 + c) * QTR

    def ship_proj(way):
        target = at_z(toward * (1 - 2 * way))
        off = quarter(way, core)
        from_ = pl.multiple_of((1 - low) * HALF + off, QTR)
        to = pl.multiple_of(off, QTR)
        go(remote(q_hbm.at[pl.ds(from_, QTR)], wq.at[1, pl.ds(to, QTR)], swq.at[way, 0], rwq.at[way, 0], target))
        go(remote(kv_hbm.at[:, pl.ds(from_, QTR)], wkv.at[1, :, pl.ds(to, QTR)], swq.at[way, 1], rwq.at[way, 1], target))

    def share_proj(way):
        to = pl.multiple_of(quarter(way, core), QTR)
        q_ref, kv_ref = wq.at[1, pl.ds(to, QTR)], wkv.at[1, :, pl.ds(to, QTR)]
        remote(q_ref, q_ref, swq.at[way, 0], rwq.at[way, 0], mate).wait_recv()
        remote(kv_ref, kv_ref, swq.at[way, 1], rwq.at[way, 1], mate).wait_recv()
        go(remote(q_ref, q_ref, swq.at[2 + way, 0], rwq.at[2 + way, 0], other_core))
        go(remote(kv_ref, kv_ref, swq.at[2 + way, 1], rwq.at[2 + way, 1], other_core))

    def shared_proj(way):
        to = pl.multiple_of(quarter(way, 1 - core), QTR)
        q_ref, kv_ref = wq.at[1, pl.ds(to, QTR)], wkv.at[1, :, pl.ds(to, QTR)]
        remote(q_ref, q_ref, swq.at[2 + way, 0], rwq.at[2 + way, 0], other_core).wait_recv()
        remote(kv_ref, kv_ref, swq.at[2 + way, 1], rwq.at[2 + way, 1], other_core).wait_recv()

    def out_part(part, c):
        start = quarter(1, c) if part == 0 else quarter(0, c) + (part - 1) * (QTR // 2)
        return start, QTR if part == 0 else QTR // 2

    def ship_out(part):
        target = at_z(toward if part == 1 else -toward)
        start, width = out_part(part, core)
        from_ = pl.multiple_of((1 - low) * HALF + start, width)
        to = pl.multiple_of(start, width)
        go(remote(out_hbm.at[:, pl.ds(from_, width)], wo.at[1, :, pl.ds(to, width)], swo.at[part], rwo.at[part], target))

    def share_out(part):
        start, width = out_part(part, core)
        ref = wo.at[1, :, pl.ds(pl.multiple_of(start, width), width)]
        remote(ref, ref, swo.at[part], rwo.at[part], mate).wait_recv()
        go(remote(ref, ref, swo.at[3 + part], rwo.at[3 + part], other_core))

    def shared_out(part):
        start, width = out_part(part, 1 - core)
        ref = wo.at[1, :, pl.ds(pl.multiple_of(start, width), width)]
        remote(ref, ref, swo.at[3 + part], rwo.at[3 + part], other_core).wait_recv()

    for load in loads:
        load.start()
    row = lax.broadcasted_iota(jnp.int32, (HB, HB), 0)
    column = lax.broadcasted_iota(jnp.int32, (HB, HB), 1)
    odd = row & column
    for bits in (4, 2, 1):
        odd = odd ^ (odd >> bits)
    signed = (1 - 2 * (odd & 1)).astype(jnp.float32).astype(jnp.bfloat16)
    for k in range(3):
        had[k * HB : (k + 1) * HB] = signed
    for copy in inputs[:3]:
        copy.wait()

    stream = resid[0].astype(jnp.float32)
    sign_row = (2 * signs[...] - 1).astype(jnp.float32)
    normed = (
        stream
        * lax.rsqrt(jnp.mean(stream * stream, axis=-1, keepdims=True) + norm_eps)
        * gain[...]
        * sign_row
    )
    per = SW // HB
    stacked = []
    for g in range(2 * NC):
        for b in range(per):
            stacked.append(
                jnp.concatenate(
                    [
                        normed[:, g * CW + j * SW + b * HB : g * CW + j * SW + (b + 1) * HB]
                        for j in range(SUB)
                    ],
                    axis=0,
                )
            )
    rotated = jnp.dot(
        split3(jnp.concatenate(stacked, axis=0)), had[...], preferred_element_type=jnp.float32
    ) * (1.0 / math.sqrt(HB))
    for g in range(2 * NC):
        blocks_of = [rotated[(g * per + b) * PR : (g * per + b + 1) * PR] for b in range(per)]
        rot[g // NC, g % NC] = jnp.concatenate(blocks_of, axis=1).astype(jnp.bfloat16)

    met(partners)

    STEP = (0, -1, 1, 2)

    def piece(h, dj, di):
        return pieces.at[h, shift(pos_y(h), dj, 4), shift(pos_x(h), di, 4)]

    def swap_copy(h):
        return remote(rot.at[1 - low], piece(h, 0, 0), sa, ra, mate)

    def spread_x(h):
        ref = piece(h, 0, 0)
        for k in (1, 2, 3):
            go(remote(ref, ref, sg2.at[h, k - 1], rg2.at[h, k - 1], ring_x(h, -STEP[k])))

    def spread_y(h, k):
        ref = piece(h, 0, STEP[k])
        for kind, by in ((0, 1), (1, -1)):
            go(remote(ref, ref, sg3.at[h, kind, k], rg3.at[h, kind, k], ring_y(h, by)))

    def from_x(h, k):
        ref = piece(h, 0, STEP[k])
        remote(ref, ref, sg2.at[h, k - 1], rg2.at[h, k - 1], mate).wait_recv()

    def from_y(h, k):
        for kind, by in ((0, -1), (1, 1)):
            ref = piece(h, by, STEP[k])
            remote(ref, ref, sg3.at[h, kind, k], rg3.at[h, kind, k], mate).wait_recv()
        by = -1 if k in (0, 3) else 1
        ref = piece(h, by, STEP[k])
        go(remote(ref, ref, sg3.at[h, 2, k], rg3.at[h, 2, k], ring_y(h, -by)))

    def from_far(h, k):
        ref = piece(h, 2, STEP[k])
        remote(ref, ref, sg3.at[h, 2, k], rg3.at[h, 2, k], mate).wait_recv()

    pieces[low, pos_y(low), pos_x(low)] = rot[low]
    go(swap_copy(low))
    ship_proj(1)
    spread_x(low)
    spread_y(low, 0)
    ship_proj(0)
    swap_copy(1 - low).wait_recv()
    spread_x(1 - low)
    spread_y(1 - low, 0)
    high_half = 1 - low
    for k in (1, 2, 3):
        from_x(low, k)
        spread_y(low, k)
    from_y(low, 0)
    for k in (1, 2, 3):
        from_x(high_half, k)
        spread_y(high_half, k)
    from_y(low, 1)
    from_y(high_half, 0)
    ship_out(0)
    ship_out(2)
    from_y(low, 2)
    from_y(high_half, 1)
    for load in loads:
        load.wait()

    def join(k):
        for h in range(2):
            i = shift(pos_x(h), STEP[k], 4)
            for c in range(NC):
                parts_of = [pieces[h, j, i, c].astype(jnp.float32) for j in range(4)]
                rows_ref[k, h, :, c * CW : (c + 1) * CW] = jnp.concatenate(
                    [
                        jnp.concatenate(
                            [part[u * ROWS : (u + 1) * ROWS] for part in parts_of], axis=0
                        )
                        for u in range(SUB)
                    ],
                    axis=1,
                ).astype(jnp.bfloat16)

    def group(k):
        return rows_ref[k].reshape(2 * PR, HALF)

    def add_own():
        part = jnp.dot(
            rows_ref[...].reshape(8 * PR, HALF), wq[0], preferred_element_type=jnp.float32
        )
        for k in range(4):
            for h in range(2):
                start = (k * 2 + h) * PR
                acc_q[h, shift(pos_x(h), STEP[k], 4)] = part[start : start + PR]

    def add_mates(k):
        part = jnp.dot(group(k), wq[1], preferred_element_type=jnp.float32)
        for h in range(2):
            cross_q[h, shift(pos_x(h), STEP[k], 4)] = part[h * PR : (h + 1) * PR].astype(
                jnp.bfloat16
            )

    def add_kv(k):
        part = lax.dot_general(
            group(k),
            wkv[...].reshape(2 * KC, HALF),
            (((1,), (1,)), ((), ())),
            preferred_element_type=jnp.float32,
        )
        for h in range(2):
            i = shift(pos_x(h), STEP[k], 4)
            acc_kv[h, i] = part[h * PR : (h + 1) * PR]
            cross_kv[h, i] = part[h * PR : (h + 1) * PR].astype(jnp.bfloat16)

    def cross_copy(kind, h, k):
        i = shift(pos_x(h), STEP[k], 4)
        src, dst = ((cross_kv, crossed_kv), (cross_q, crossed_q))[kind]
        return remote(src.at[h, i], dst.at[h, i], scr.at[kind, h, k], rcr.at[kind, h, k], mate)

    def cross_group(k):
        add_kv(k)
        for h in range(2):
            go(cross_copy(0, h, k))
        add_mates(k)
        for h in range(2):
            go(cross_copy(1, h, k))

    for copy in inputs[3:]:
        copy.wait()
    tok_cos = table.at[: HD // 2, :TOK]
    tok_sin = table.at[: HD // 2, TOK : 2 * TOK]
    query_tok = table.at[HD // 2 : HD // 2 + 1, : 2 * TOK]
    inverse = table.at[: HD // 2, 2 * TOK :]
    key_tok[...] = jnp.transpose(
        jnp.broadcast_to(table[HD // 2 : HD // 2 + 1, :TOK], (HB, TOK))
    )
    lane = lax.broadcasted_iota(jnp.int32, (1, HB), 1)
    starts = jnp.zeros((1, HB), jnp.int32)
    for b in range(BLOCKS - 1):
        starts = starts + jnp.where(lane > b, lengths[b], 0)
    angles = inverse[...] * starts.astype(jnp.float32)
    off_cos[...] = jnp.cos(angles)
    off_sin[...] = jnp.sin(angles)

    def rotary_table(index):
        here_only = lane == index
        oc = jnp.sum(jnp.where(here_only, off_cos[...], 0.0), axis=1, keepdims=True)
        os = jnp.sum(jnp.where(here_only, off_sin[...], 0.0), axis=1, keepdims=True)
        return oc * tok_cos[...] - os * tok_sin[...], os * tok_cos[...] + oc * tok_sin[...]

    def own_group(k):
        for h in range(2):
            from_far(h, k)
        join(k)

    own_group(0)
    from_y(low, 3)
    from_y(high_half, 2)
    share_proj(1)
    share_proj(0)
    ship_out(1)
    own_group(1)
    for way in range(2):
        shared_proj(way)
    cross_group(0)
    from_y(high_half, 3)
    cross_group(1)
    own_group(2)
    cross_group(2)
    for h in range(2):
        from_far(h, 3)
    join(3)
    cross_group(3)
    half = HD // 2

    def side(e):
        return own_x if e == 0 else 1 - own_x

    def kv_piece(e, by):
        return kvs.at[core, side(e), shift(z, by, 8)]

    def along(by, hops, kind):
        ref = kv_piece(0, by)
        return remote(ref, ref, skv.at[kind], rkv.at[kind], at_z(hops))

    def across(by, hops, kind):
        ref = kv_piece(0, by)
        return remote(ref, ref, sx.at[kind], rx.at[kind], x_mate_at(hops))

    def to_mates(by, x_too=True):
        ref = kv_piece(0, by)
        k = by % 8
        if x_too:
            go(remote(ref, ref, sx.at[k], rx.at[k], x_mate))
        go(remote(ref, ref, sc.at[0, k], rc.at[0, k], other_core))

    def from_x_mate(by):
        ref = kv_piece(1, by)
        k = by % 8
        remote(ref, ref, sx.at[k], rx.at[k], x_mate).wait_recv()
        go(remote(ref, ref, sc.at[1, k], rc.at[1, k], other_core))

    for k in range(4):
        for h in range(2):
            cross_copy(0, h, k).wait_recv()
    kv_sum = acc_kv[...].reshape(TOK, 2 * KC) + pltpu.roll(
        crossed_kv[...].astype(jnp.float32).reshape(TOK, 2 * KC), KC, 1
    )
    kvs[core, own_x, z] = jnp.transpose(kv_sum)[:KC].astype(jnp.bfloat16)
    go(along(0, 2, 2))
    go(along(0, -2, 3))
    go(along(0, 1, 0))
    go(along(0, -1, 1))
    to_mates(0)
    add_own()

    for k in range(4):
        for h in range(2):
            cross_copy(1, h, k).wait_recv()
    turned = jnp.transpose(
        (acc_q[...] + crossed_q[...].astype(jnp.float32)).reshape(TOK, QC)
    )
    cosine, sine = rotary_table(section)
    for head in range(2):
        first = turned[head * HD : head * HD + half]
        second = turned[head * HD + half : (head + 1) * HD]
        queries[:half, head * TOK : (head + 1) * TOK] = (
            first * cosine - second * sine
        ).astype(jnp.bfloat16)
        queries[half:, head * TOK : (head + 1) * TOK] = (
            second * cosine + first * sine
        ).astype(jnp.bfloat16)

    def from_core(back):
        for u in range(2):
            k = shift(u - low, 8 - 2 * back, 8)
            for e in range(2):
                ref = kvs.at[1 - core, side(e), lax.rem(z + k, 8)]
                remote(ref, ref, sc.at[e, k], rc.at[e, k], other_core).wait_recv()

    scale = math.log2(math.e) / math.sqrt(HD)

    def absorb(c, row, diagonal):
        index = row * 2 + c
        pair = pl.ds(row * 2, 2)
        raw = kvs[c, 0, pair].astype(jnp.float32)
        value = kvs[c, 1, pair].reshape(HD, TOK)
        cosine, sine = rotary_table(index)
        key = jnp.concatenate(
            [raw[0] * cosine - raw[1] * sine, raw[1] * cosine + raw[0] * sine], axis=0
        )
        key = jnp.transpose(key).astype(jnp.bfloat16)
        scores = jnp.dot(key, queries[...], preferred_element_type=jnp.float32)
        token = key_tok[:, :1]
        valid = token < lengths[index].astype(jnp.float32)
        if diagonal:
            seen = valid & (token <= query_tok[...])
            scores = jnp.where(seen, scores, NEG)
            top = jnp.max(scores, axis=0, keepdims=True)
            weights = jnp.exp2((scores - top) * scale)
            total_ref[...] = jnp.sum(weights, axis=0, keepdims=True)
            acc[...] = jnp.dot(
                value, weights.astype(jnp.bfloat16), preferred_element_type=jnp.float32
            )
        else:
            scores = scores + jnp.where(valid, 0.0, NEG)
            old = top_ref[...]
            top = jnp.maximum(old, jnp.max(scores, axis=0, keepdims=True))
            weights = jnp.exp2((scores - top) * scale)
            fade = jnp.exp2((old - top) * scale)
            total_ref[...] = total_ref[...] * fade + jnp.sum(weights, axis=0, keepdims=True)
            acc[...] = acc[...] * fade + jnp.dot(
                value, weights.astype(jnp.bfloat16), preferred_element_type=jnp.float32
            )
        top_ref[...] = top

    def earlier(back):
        @pl.when(high >= back)
        def _():
            for c in range(2):
                absorb(c, high - back, False)

    for by, kind in ((-2, 2), (2, 3)):
        along(by, 0, kind).wait_recv()
        on = 1 if by < 0 else -1
        go(along(by, on, 4 if by < 0 else 5))
        go(across(by, on, (by - on) % 8))
        to_mates(by)
    turn = 2 - 4 * core
    go(along(-turn, turn, 6))
    go(across(-turn, turn, 4))
    for by, kind in ((-1, 0), (1, 1)):
        along(by, 0, kind).wait_recv()
        to_mates(by)
    for by in (0, -2, 2, -1, 1):
        from_x_mate(by)
    for by, kind in ((-3, 4), (3, 5), (4, 6)):
        along(by, 0, kind).wait_recv()
        to_mates(by, False)
    from_core(0)
    absorb(core, high, True)

    @pl.when(core == 1)
    def _():
        absorb(0, high, False)

    for part in range(3):
        share_out(part)
    for by in (-3, 3, 4):
        from_x_mate(by)
    near = 1 + 2 * low
    for back in (near, 4 - near, 2):
        from_core(back)
        earlier(back)
    attended = acc[...] / total_ref[...]
    for head in range(2):
        rows = jnp.transpose(attended[:, head * TOK : (head + 1) * TOK])
        for h in range(2):
            for j in range(4):
                att[0, h, j, :, head * HD : (head + 1) * HD] = jnp.concatenate(
                    [
                        rows[h * 4 * PR + i * PR + j * ROWS : h * 4 * PR + i * PR + (j + 1) * ROWS]
                        for i in range(4)
                    ],
                    axis=0,
                ).astype(jnp.bfloat16)
    def att_copy(h, k):
        j = shift(pos_y(h), FAR_FIRST[k], 4)
        return remote(att.at[0, h, j], att.at[1, h, j], sat.at[h, k], rat.at[h, k], mate)

    FAR_FIRST = (2, 1, -1, 0)
    for k in range(4):
        for h in range(2):
            go(att_copy(h, k))
    for part in range(3):
        shared_out(part)

    def send_raw(buf, raw, fin, pos, ssem, rsem, peer, h, c):
        by = 1 if c % 2 == 0 else -1
        go(
            remote(
                buf.at[h, shift(pos(h), 2, 4), c], raw.at[h, c], ssem.at[h, 2, c],
                rsem.at[h, 2, c], peer(h, by),
            )
        )

    def send_fin(buf, raw, fin, pos, ssem, rsem, peer, h, c, kind):
        by = 1 if kind == 0 else -1
        go(
            remote(
                buf.at[h, shift(pos(h), by, 4), c], fin.at[h, kind, c], ssem.at[h, kind, c],
                rsem.at[h, kind, c], peer(h, by),
            )
        )

    def pass_on(buf, raw, fin, pos, ssem, rsem, peer, h, c):
        kind, by = (0, 1) if c % 2 == 0 else (1, -1)
        ref = raw.at[h, c]
        remote(ref, ref, ssem.at[h, 2, c], rsem.at[h, 2, c], peer(h, 1)).wait_recv()
        slot = shift(pos(h), by, 4)
        buf[h, slot, c] = (
            buf[h, slot, c].astype(jnp.float32) + raw[h, c].astype(jnp.float32)
        ).astype(jnp.bfloat16)
        send_fin(buf, raw, fin, pos, ssem, rsem, peer, h, c, kind)

    def finish(buf, raw, fin, pos, ssem, rsem, peer, h, c):
        for kind in range(2):
            ref = fin.at[h, kind, c]
            remote(ref, ref, ssem.at[h, kind, c], rsem.at[h, kind, c], peer(h, 1)).wait_recv()
        return (
            buf[h, pos(h), c].astype(jnp.float32)
            + fin[h, 0, c].astype(jnp.float32)
            + fin[h, 1, c].astype(jnp.float32)
        )

    ring1 = (parts, raw1, fin1, pos_y, s1, r1, ring_y)

    def scatter_x(c):
        for k in range(4):
            i = shift(pos_x(low), -STEP[k], 4)
            j = shift(pos_x(1 - low), -STEP[k], 4)
            near_chip = ring_x(low, -STEP[k])
            far_chip = beyond(-STEP[k])
            if k > 0:
                go(
                    remote(
                        parts2.at[low, i, c], fin2.at[0, k, c], s2.at[0, k, c], r2.at[0, k, c], near_chip
                    )
                )
            go(
                remote(
                    parts2.at[1 - low, j, c], fin2.at[1, k, c], s2.at[1, k, c], r2.at[1, k, c], far_chip
                )
            )

    def sum_x(where, c):
        done = parts2[low, pos_x(low), c].astype(jnp.float32) if where == 0 else None
        for k in range(4):
            if where == 0 and k == 0:
                continue
            ref = fin2.at[where, k, c]
            remote(ref, ref, s2.at[where, k, c], r2.at[where, k, c], mate).wait_recv()
            term = fin2[where, k, c].astype(jnp.float32)
            done = term if done is None else done + term
        return done

    sign_row = (2 * signs[...] - 1).astype(jnp.float32)

    def close(c):
        full[low] = sum_x(0, c)
        full[1 - low] = sum_x(1, c)
        stacked = []
        for g in range(2):
            branch = full[g]
            stacked += [branch[:, b * HB : (b + 1) * HB] for b in range(per)]
        back = jnp.dot(
            split3(jnp.concatenate(stacked, axis=0)), had[...], preferred_element_type=jnp.float32
        ) * (1.0 / math.sqrt(HB))
        for g in range(2):
            at = slice(g * HALF + c * CW, g * HALF + (c + 1) * CW)
            pieces_of = []
            for j in range(SUB):
                for b in range(per):
                    row = (g * per + b) * PR + j * ROWS
                    pieces_of.append(back[row : row + ROWS])
            mixed[0, :, at] = (
                resid[0, :, at].astype(jnp.float32)
                + sign_row[:, at] * jnp.concatenate(pieces_of, axis=1)
            ).astype(jnp.bfloat16)

    def out_rows(ks, c):
        columns = pl.ds(c * CW, CW)
        spots = [(h, shift(pos_y(h), FAR_FIRST[k], 4)) for k in ks for h in range(2)]
        total = None
        for kind in range(2):
            left = jnp.concatenate([att[kind, h, j] for h, j in spots], axis=0)
            term = jnp.dot(left, wo[kind, :, columns], preferred_element_type=jnp.float32)
            total = term if total is None else total + term
        for n, (h, j) in enumerate(spots):
            parts[h, j, c] = total[n * PR : (n + 1) * PR].astype(jnp.bfloat16)

    for h in range(2):
        att_copy(h, 0).wait_recv()
    for c in range(NC):
        out_rows((0,), c)
        for h in range(2):
            send_raw(*ring1, h, c)
    for k in (1, 2, 3):
        for h in range(2):
            att_copy(h, k).wait_recv()
    for c0 in (0, 2):
        for c in (c0, c0 + 1):
            out_rows((1, 2, 3), c)
            for h in range(2):
                send_fin(*ring1, h, c, 1 if c % 2 == 0 else 0)
        for c in (c0, c0 + 1):
            for h in range(2):
                pass_on(*ring1, h, c)
    for c in range(NC):
        for h in range(2):
            done = finish(*ring1, h, c)
            for i in range(4):
                parts2[h, i, c] = jnp.concatenate(
                    [
                        done[i * ROWS : (i + 1) * ROWS, j * SW : (j + 1) * SW]
                        for j in range(SUB)
                    ],
                    axis=0,
                ).astype(jnp.bfloat16)
        scatter_x(c)
        if c > 0:
            close(c - 1)
    close(NC - 1)
    for copy in started:
        copy.wait_send()


def vmem(shape, dtype):
    return pltpu.VMEM(shape, dtype)


def shards(resid, norm_gain, signs, query_weight, kv_weight, out_weight, lengths):
    bf16, f32 = jnp.bfloat16, jnp.float32
    dma = pltpu.SemaphoreType.DMA
    in_vmem = pl.BlockSpec(memory_space=pltpu.VMEM)
    in_hbm = pl.BlockSpec(memory_space=pltpu.HBM)
    order = token_order()
    inverse = np.exp(np.arange(HD // 2) * (-2.0 * math.log(rope_base) / HD))
    angles = inverse[:, None] * order[None, :]
    table = np.zeros((HD // 2 + 8, 2 * TOK + HB))
    table[: HD // 2, :TOK] = np.cos(angles)
    table[: HD // 2, TOK : 2 * TOK] = np.sin(angles)
    table[HD // 2, : 2 * TOK] = np.concatenate([order, order])
    table[: HD // 2, 2 * TOK :] = inverse[:, None]
    ring = dma((2, 3, NC))
    return pl.pallas_call(
        sublayer_kernel,
        out_shape=jax.ShapeDtypeStruct(resid.shape, bf16),
        in_specs=[in_hbm] * 8,
        out_specs=in_vmem,
        scratch_shapes=[
            pltpu.SMEM((BLOCKS,), jnp.int32),
            vmem(resid.shape, bf16),
            vmem((1, D), f32),
            vmem((1, D), jnp.int32),
            vmem(table.shape, f32),
            vmem((3 * HB, HB), bf16),
            vmem((TOK, HB), f32),
            vmem((2, HALF, QC), bf16),
            vmem((2, KC, HALF), bf16),
            vmem((2, QC, HALF), bf16),
            vmem((2, NC, PR, SW), bf16),
            vmem((2, 4, 4, NC, PR, SW), bf16),
            vmem((4, 2, PR, HALF), bf16),
            vmem((2, 4, PR, QC), f32),
            vmem((2, 4, PR, 2 * KC), f32),
            vmem((2, 4, PR, QC), bf16),
            vmem((2, 4, PR, 2 * KC), bf16),
            vmem((2, 4, PR, QC), bf16),
            vmem((2, 4, PR, 2 * KC), bf16),
            vmem((HD, 2 * TOK), bf16),
            vmem((HD // 2, HB), f32),
            vmem((HD // 2, HB), f32),
            vmem((2, 2, 8, KC, TOK), bf16),
            vmem((1, 2 * TOK), f32),
            vmem((1, 2 * TOK), f32),
            vmem((HD, 2 * TOK), f32),
            vmem((2, 2, 4, PR, QC), bf16),
            vmem((2, 4, NC, PR, CW), bf16),
            vmem((2, NC, PR, CW), bf16),
            vmem((2, 2, NC, PR, CW), bf16),
            vmem((2, 4, NC, PR, SW), bf16),
            vmem((2, 4, NC, PR, SW), bf16),
            vmem((2, PR, SW), f32),
            dma((5,)),
            dma((3,)),
            dma((4, 2)),
            dma((4, 2)),
            dma((6,)),
            dma((6,)),
            dma,
            dma,
            dma((2, 3)),
            dma((2, 3)),
            dma((2, 3, 4)),
            dma((2, 3, 4)),
            dma((2, 2, 4)),
            dma((2, 2, 4)),
            dma((8,)),
            dma((8,)),
            dma((7,)),
            dma((7,)),
            dma((2, 8)),
            dma((2, 8)),
            dma((2, 4)),
            dma((2, 4)),
            ring,
            ring,
            dma((2, 4, NC)),
            dma((2, 4, NC)),
        ],
        compiler_params=pltpu.CompilerParams(
            collective_id=1, has_side_effects=True, vmem_limit_bytes=60 << 20
        ),
        name="sublayer",
    )(
        lengths, resid, norm_gain[None, :], signs[None, :], jnp.asarray(table, f32),
        query_weight, kv_weight.T, out_weight,
    )


def solution(mesh):
    return jax.shard_map(
        shards,
        mesh=mesh,
        in_specs=(
            P("section", "tensor", None),
            P(),
            P(),
            P(None, "tensor"),
            P(None, "tensor"),
            P("tensor", None),
            P(),
        ),
        out_specs=P("section", "tensor", None),
        check_vma=False,
    )
```

time: 109 us -> 92.3 us (0.85)
  local copies, waits for them, and re-layouts: 10.1 us -> 1.67 us
  Pallas kernels: 98.8 us -> 90.5 us
    unnamed x23 -> x1, local copies, waits for them, and re-layouts: 10.1 us -> 1.67 us
    pallas_call x1, Pallas kernels: 98.8 us -> 90.5 us  [shards(): pl.pallas_call(sublayer_kernel, out_shape=jax.ShapeDtypeStruct(resid.shap...]
where the time goes in v3:
time: 92.3 us; the launch traced here: 92.2 us
  Pallas kernels  90.5 us (98%)
  local copies, waits for them, and re-layouts  1.67 us (2%)
    pallas_call x1, Pallas kernels, shards(): pl.pallas_call(sublayer_kernel, out_shape=jax.ShapeDtypeStruct(resid.shap...  90.5 us

profile of v3, /device:TPU:192, one launch (start us, length us, event | category | flops | bytes accessed | tf_op | source)
XLA Modules:
  0.0 92.2 jit_solution(14262417694709811639)
XLA Ops:
  0.0 90.5 %sublayer.1 = bf16[1,12,8192]{2,1,0:T(8,128)(2,1)} custom-call(s32[8]{0:T(128)} %lengths_hbm.1, bf16[1,12,8192]{2,1,0:T(8,128)(2,1)} %resid_hbm.1, f32[1,8192]{1,0:T(1,128)} %bitcast.4, s32[1,8192]{1,0:T(1,128)} %bitcast.5, f32[72,896]{1,0:T(8,128)} %constant.2.clone.table_hbm, bf16[8192,256]{1,0:T(8,128)(2,1)} %q_hbm.1, bf16[64,8192]{1,0:T(8,128)(2,1)} %bitcast.3, ...), custom_call_target="tpu_custom_call" | custom-call | tf_op jit(solution)/shard_map/sublayer/pallas_call | solution.py:749
  90.5 1.7 %copy.10 = bf16[1,12,8192]{2,1,0:T(8,128)(2,1)} copy(bf16[1,12,8192]{2,1,0:T(8,128)(2,1)} %sublayer.1) | data formatting | bytes 393216

commit v4 on v3

--- a/solution.py
+++ b/solution.py
@@ -16,7 +16,7 @@
 ROWS = 12
 TOK = 384
 BLOCKS = 8
-NC = 4
+NC = 2
 HALF = D // 2
 CW = HALF // NC
 SUB = 4
@@ -89,7 +89,7 @@
 def sublayer_kernel(
     lengths_hbm, resid_hbm, gain_hbm, signs_hbm, table_hbm, q_hbm, kv_hbm, out_hbm, mixed,
     lengths, resid, gain, signs, table, had, key_tok, wq, wkv, wo, rot, pieces, rows_ref, acc_q, acc_kv, cross_q, cross_kv, crossed_q, crossed_kv, queries, off_cos, off_sin,
-    kvs, top_ref, total_ref, acc, att, parts, raw1, fin1, parts2, fin2, full,
+    kvs, top_ref, total_ref, acc, att, parts, raw1, fin1, parts2, fin2, sums, last_z, own_sum, full,
     in_sem, w_sem, swq, rwq, swo, rwo, sa, ra, sg2, rg2, sg3, rg3, scr, rcr, sx, rx, skv, rkv, sc, rc,
     sat, rat, s1, r1, s2, r2,
 ):
@@ -135,18 +135,13 @@
         copy.start()
         started.append(copy)
 
-    def beyond(by):
-        h = 1 - low
-        return device(shift(y, by * h, 4), shift(x, by * (1 - h), 4), shift(z, toward, 8), core)
-
-    def behind(by):
-        return device(
-            shift(y, by * low, 4), shift(x, by * (1 - low), 4), shift(z, toward, 8), core
-        )
+    def settle():
+        for copy in started:
+            copy.wait_send()
+        started.clear()
 
     partners = [at_z(by) for by in (1, -1, 2, -2)] + [other_core]
     partners += [at_x(by) for by in (1, -1, 2)] + [at_y(by) for by in (1, -1, 2)]
-    partners += [behind(by) for by in (1, -1, 2)]
     partners += [x_mate_at(by) for by in (1, -1, 2, -2)]
     greet(partners)
     inputs = [
@@ -346,12 +341,16 @@
                 start = (k * 2 + h) * PR
                 acc_q[h, shift(pos_x(h), STEP[k], 4)] = part[start : start + PR]
 
-    def add_mates(k):
-        part = jnp.dot(group(k), wq[1], preferred_element_type=jnp.float32)
-        for h in range(2):
-            cross_q[h, shift(pos_x(h), STEP[k], 4)] = part[h * PR : (h + 1) * PR].astype(
-                jnp.bfloat16
-            )
+    def add_mates(first):
+        rows = rows_ref[first : first + 2].reshape(4 * PR, HALF)
+        part = jnp.dot(rows, wq[1], preferred_element_type=jnp.float32)
+        for k in (first, first + 1):
+            for h in range(2):
+                start = ((k - first) * 2 + h) * PR
+                cross_q[h, shift(pos_x(h), STEP[k], 4)] = part[start : start + PR].astype(
+                    jnp.bfloat16
+                )
+                go(cross_copy(1, h, k))
 
     def add_kv(k):
         part = lax.dot_general(
@@ -374,9 +373,6 @@
         add_kv(k)
         for h in range(2):
             go(cross_copy(0, h, k))
-        add_mates(k)
-        for h in range(2):
-            go(cross_copy(1, h, k))
 
     for copy in inputs[3:]:
         copy.wait()
@@ -418,12 +414,14 @@
     cross_group(0)
     from_y(high_half, 3)
     cross_group(1)
+    add_mates(0)
     own_group(2)
     cross_group(2)
     for h in range(2):
         from_far(h, 3)
     join(3)
     cross_group(3)
+    add_mates(2)
     half = HD // 2
 
     def side(e):
@@ -547,22 +545,24 @@
         to_mates(by)
     for by in (0, -2, 2, -1, 1):
         from_x_mate(by)
+    from_core(0)
+    absorb(core, high, True)
+
+    @pl.when(core == 1)
+    def _():
+        absorb(0, high, False)
+
+    near = 1 + 2 * low
+    from_core(near)
+    earlier(near)
     for by, kind in ((-3, 4), (3, 5), (4, 6)):
         along(by, 0, kind).wait_recv()
         to_mates(by, False)
-    from_core(0)
-    absorb(core, high, True)
-
-    @pl.when(core == 1)
-    def _():
-        absorb(0, high, False)
-
+    for by in (-3, 3, 4):
+        from_x_mate(by)
     for part in range(3):
         share_out(part)
-    for by in (-3, 3, 4):
-        from_x_mate(by)
-    near = 1 + 2 * low
-    for back in (near, 4 - near, 2):
+    for back in (4 - near, 2):
         from_core(back)
         earlier(back)
     attended = acc[...] / total_ref[...]
@@ -629,39 +629,37 @@
     ring1 = (parts, raw1, fin1, pos_y, s1, r1, ring_y)
 
     def scatter_x(c):
-        for k in range(4):
-            i = shift(pos_x(low), -STEP[k], 4)
-            j = shift(pos_x(1 - low), -STEP[k], 4)
-            near_chip = ring_x(low, -STEP[k])
-            far_chip = beyond(-STEP[k])
-            if k > 0:
+        for h in range(2):
+            for k in (1, 2, 3):
                 go(
                     remote(
-                        parts2.at[low, i, c], fin2.at[0, k, c], s2.at[0, k, c], r2.at[0, k, c], near_chip
+                        parts2.at[h, shift(pos_x(h), -STEP[k], 4), c], fin2.at[h, k, c],
+                        s2.at[h, k, c], r2.at[h, k, c], ring_x(h, -STEP[k]),
                     )
                 )
-            go(
-                remote(
-                    parts2.at[1 - low, j, c], fin2.at[1, k, c], s2.at[1, k, c], r2.at[1, k, c], far_chip
-                )
-            )
-
-    def sum_x(where, c):
-        done = parts2[low, pos_x(low), c].astype(jnp.float32) if where == 0 else None
-        for k in range(4):
-            if where == 0 and k == 0:
-                continue
-            ref = fin2.at[where, k, c]
-            remote(ref, ref, s2.at[where, k, c], r2.at[where, k, c], mate).wait_recv()
-            term = fin2[where, k, c].astype(jnp.float32)
-            done = term if done is None else done + term
+
+    def sum_x(h, c):
+        done = parts2[h, pos_x(h), c].astype(jnp.float32)
+        for k in (1, 2, 3):
+            ref = fin2.at[h, k, c]
+            remote(ref, ref, s2.at[h, k, c], r2.at[h, k, c], mate).wait_recv()
+            done = done + fin2[h, k, c].astype(jnp.float32)
         return done
 
+    def z_copy(c):
+        return remote(sums.at[c], last_z.at[c], s2.at[0, 0, c], r2.at[0, 0, c], mate)
+
+    def swap(c):
+        sums[c] = sum_x(1 - low, c).astype(jnp.bfloat16)
+        go(z_copy(c))
+        own_sum[c] = sum_x(low, c)
+
     sign_row = (2 * signs[...] - 1).astype(jnp.float32)
 
     def close(c):
-        full[low] = sum_x(0, c)
-        full[1 - low] = sum_x(1, c)
+        z_copy(c).wait_recv()
+        full[low] = own_sum[c]
+        full[1 - low] = last_z[c].astype(jnp.float32)
         stacked = []
         for g in range(2):
             branch = full[g]
@@ -692,16 +690,20 @@
         for n, (h, j) in enumerate(spots):
             parts[h, j, c] = total[n * PR : (n + 1) * PR].astype(jnp.bfloat16)
 
+    early = list(started)
+    started.clear()
     for h in range(2):
         att_copy(h, 0).wait_recv()
     for c in range(NC):
         out_rows((0,), c)
         for h in range(2):
             send_raw(*ring1, h, c)
+    for copy in early:
+        copy.wait_send()
     for k in (1, 2, 3):
         for h in range(2):
             att_copy(h, k).wait_recv()
-    for c0 in (0, 2):
+    for c0 in range(0, NC, 2):
         for c in (c0, c0 + 1):
             out_rows((1, 2, 3), c)
             for h in range(2):
@@ -720,12 +722,20 @@
                     ],
                     axis=0,
                 ).astype(jnp.bfloat16)
+        if c == NC - 1:
+            early = list(started)
+            started.clear()
         scatter_x(c)
         if c > 0:
-            close(c - 1)
+            swap(c - 1)
+        if c > 1:
+            close(c - 2)
+    for copy in early:
+        copy.wait_send()
+    swap(NC - 1)
+    close(NC - 2)
     close(NC - 1)
-    for copy in started:
-        copy.wait_send()
+    settle()
 
 
 def vmem(shape, dtype):
@@ -784,6 +794,9 @@
             vmem((2, 2, NC, PR, CW), bf16),
             vmem((2, 4, NC, PR, SW), bf16),
             vmem((2, 4, NC, PR, SW), bf16),
+            vmem((NC, PR, SW), bf16),
+            vmem((NC, PR, SW), bf16),
+            vmem((NC, PR, SW), f32),
             vmem((2, PR, SW), f32),
             dma((5,)),
             dma((3,)),

time: 92.3 us -> 89 us (0.964)
  Pallas kernels: 90.5 us -> 87.2 us
    pallas_call x1, Pallas kernels: 90.5 us -> 87.2 us  [shards(): pl.pallas_call(sublayer_kernel, out_shape=jax.ShapeDtypeStruct(resid.shap...]
where the time goes in v4:
time: 89 us; the launch traced here: 88.9 us
  Pallas kernels  87.2 us (98%)
  local copies, waits for them, and re-layouts  1.67 us (2%)
    pallas_call x1, Pallas kernels, shards(): pl.pallas_call(sublayer_kernel, out_shape=jax.ShapeDtypeStruct(resid.shap...  87.2 us

profile of v4, /device:TPU:192, one launch (start us, length us, event | category | flops | bytes accessed | tf_op | source)
XLA Modules:
  0.0 88.9 jit_solution(4643608646319233806)
XLA Ops:
  0.0 87.2 %sublayer.1 = bf16[1,12,8192]{2,1,0:T(8,128)(2,1)} custom-call(s32[8]{0:T(128)} %lengths_hbm.1, bf16[1,12,8192]{2,1,0:T(8,128)(2,1)} %resid_hbm.1, f32[1,8192]{1,0:T(1,128)} %bitcast.4, s32[1,8192]{1,0:T(1,128)} %bitcast.5, f32[72,896]{1,0:T(8,128)} %constant.2.clone.table_hbm, bf16[8192,256]{1,0:T(8,128)(2,1)} %q_hbm.1, bf16[64,8192]{1,0:T(8,128)(2,1)} %bitcast.3, ...), custom_call_target="tpu_custom_call" | custom-call | tf_op jit(solution)/shard_map/sublayer/pallas_call | solution.py:759
  87.2 1.7 %copy.10 = bf16[1,12,8192]{2,1,0:T(8,128)(2,1)} copy(bf16[1,12,8192]{2,1,0:T(8,128)(2,1)} %sublayer.1) | data formatting | bytes 393216
